TPU v7x, 512 devices: a whole 4x8x8 slice. The times are simulated.
512 devices in a mesh: blk: 64 (over z_lo, y, core), fsdp: 8 (over x, z_hi).
Axes of the slice: x: 4, y: 8, z: 8 (z_hi: 2, z_lo: 4; z = z_hi * 4 + z_lo), core: 2. Of those that a mesh axis runs over, the one named last changes fastest.
Arguments:
- params: float32 [64, 128, 5120], P('blk', 'fsdp'), may hold values from -6.5 to 6.5
- public: float32 [64, 128, 5120], P('blk', 'fsdp'), may hold values from -16 to 16
- mixed: float32 [64, 128, 5120], P('blk', 'fsdp'), may hold values from -16 to 16
- hidden: bfloat16 [64, 2, 1024, 128], P('blk', None, 'fsdp'), may hold values from -6 to 6
- cotangent: bfloat16 [64, 2, 1024, 5120], P('blk', None, 'fsdp'), may hold values from -0.1875 to 0.1875
Outputs:
- new_params: float32 [64, 128, 5120], P('blk', 'fsdp')
- new_public: float32 [64, 128, 5120], P('blk', 'fsdp')
- new_mixed: float32 [64, 128, 5120], P('blk', 'fsdp')
All inputs are finite; a program needn't handle non-finite values.
Results may differ from a plain program's by a relative error of at most 0.007.
Values may be sent and summed in bfloat16 or wider, within the bound.
A program may use at most 64 MiB of HBM per device.

v0:
```python
import jax
import jax.numpy as jnp
from jax import lax
from jax.sharding import PartitionSpec as P

BLOCK = 32


LEARN_RATE = 0.25
MIX_RATE = 0.4
SCALE_FLOOR = 0.25
CODE_LIMIT = 2.0


def passed_along(block, axis, distance):
    devices = range(lax.axis_size(axis))
    route = [((i - distance) % len(devices), i) for i in devices]
    return lax.ppermute(block, axis, route)


def block_table(feature_count):
    column = lax.broadcasted_iota(jnp.int32, (feature_count, feature_count // BLOCK), 0) // BLOCK
    block_id = lax.broadcasted_iota(jnp.int32, (feature_count, feature_count // BLOCK), 1)
    return (column == block_id).astype(jnp.float32)


def spread_out(scales, pooling):
    return lax.dot_general(
        scales.astype(jnp.float32),
        pooling,
        (((1,), (1,)), ((), ())),
        precision=lax.Precision.HIGHEST,
        preferred_element_type=jnp.float32,
    )


def encode(change, pooling):
    energy = lax.dot_general(
        change * change,
        pooling,
        (((1,), (0,)), ((), ())),
        precision=lax.Precision.HIGHEST,
        preferred_element_type=jnp.float32,
    )
    scales = jnp.maximum(jnp.sqrt(energy * (1.0 / BLOCK)), SCALE_FLOOR).astype(jnp.bfloat16)
    wide_scale = spread_out(lax.optimization_barrier(scales), pooling)
    encoded = jnp.clip(change / wide_scale, -CODE_LIMIT, CODE_LIMIT).astype(jnp.bfloat16)
    return (encoded, scales, wide_scale)


def decode(encoded, scales, pooling):
    return encoded.astype(jnp.float32) * spread_out(scales, pooling)


def round_term(acts_now, cots_now):
    return lax.dot_general(
        acts_now, cots_now, (((0,), (0,)), ((), ())), preferred_element_type=jnp.float32
    )


def per_device(params, public, mixed, hidden, cotangent):
    weights = params[0]
    shared = public[0]
    blended = mixed[0]
    activations = hidden[0]
    cotangents = cotangent[0]
    rounds = activations.shape[0]
    pooling = block_table(weights.shape[1])
    for round_index in range(rounds):
        gradient = lax.psum_scatter(
            round_term(activations[round_index], cotangents[round_index]).astype(jnp.bfloat16),
            "fsdp",
            scatter_dimension=0,
            tiled=True,
        ).astype(jnp.float32)
        stepped = weights - LEARN_RATE * gradient
        encoded, scales, wide_scale = encode(stepped - shared, pooling)
        message = encoded.astype(jnp.float32) * wide_scale
        left_pair = passed_along((encoded, scales), "blk", 1)
        right_pair = passed_along((encoded, scales), "blk", -1)
        from_left = decode(left_pair[0], left_pair[1], pooling)
        from_right = decode(right_pair[0], right_pair[1], pooling)
        shared = shared + message
        blended = blended + (message + from_left + from_right) / 3.0
        weights = stepped + MIX_RATE * (blended - shared)
    return (weights[None], shared[None], blended[None])


def solution(mesh):
    placed = (
        P("blk", "fsdp", None),
        P("blk", "fsdp", None),
        P("blk", "fsdp", None),
        P("blk", None, "fsdp", None),
        P("blk", None, "fsdp", None),
    )
    return jax.shard_map(
        per_device,
        mesh=mesh,
        in_specs=placed,
        out_specs=(P("blk", "fsdp", None), P("blk", "fsdp", None), P("blk", "fsdp", None)),
        check_vma=False,
    )
```

profile of v0, /device:TPU:6, one launch (start us, length us, event | category | flops | bytes accessed | tf_op | source)
XLA Modules:
  0.0 244.4 jit_solution(3085147365913694608)
XLA Ops:
  7.2 0.0 copy-start
  7.2 0.0 copy-start.4
  7.2 0.0 reduce-scatter.3.cloned.1.call-start
  7.2 3.1 %convolution_convert_fusion.1 = bf16[128,5120]{1,0:T(8,128)(2,1)} fusion(bf16[1,2,128,5120]{3,2,1,0:T(8,128)(2,1)} %param.9, bf16[1,2,128,128]{3,2,1,0:T(8,128)(2,1)} %param.8), kind=kOutput, calls=%fused_computation.1 | convolution fusion | flops 168427520 | bytes 2654208 | tf_op jit(solution)/shard_map/dot_general | solution.py:56
  10.3 0.0 copy-start.1
  10.3 0.0 copy-start.5
  10.3 0.0 reduce-scatter.3.cloned.1.call-update
  10.3 0.0 reduce-scatter.5.cloned.1.call-start
  10.4 0.0 copy-done
  10.4 0.0 copy-done.4
  10.4 1.6 convolution_convert_fusion
  12.0 0.0 reduce-scatter.5.cloned.1.call-update
  12.1 100.1 %reduce-scatter.3.cloned.1.call-done = bf16[16,5120]{1,0:T(8,128)(2,1)} async-done(((bf16[128,5120]{1,0:T(8,128)(2,1)}), bf16[16,5120]{1,0:T(8,128)(2,1)}) %reduce-scatter.3.cloned.1.call-update) | async-done | bytes 163856 | tf_op jit(solution)/shard_map/reduce_scatter | solution.py:70
  112.2 0.0 copy-start.2
  112.2 0.0 copy-done.1
  112.2 0.0 copy-done.5
  112.2 2.6 %fusion.43 = bf16[16,160]{1,0:T(8,128)(2,1)S(1)} fusion(s32[5120]{0:T(1024)S(1)} %get-tuple-element.12, s32[5120]{0:T(1024)S(1)} %get-tuple-element.13, pred[5120]{0:T(1024)(128)(4,1)S(1)} %fusion.54, f32[1,16,5120]{2,1,0:T(8,128)S(1)} %copy-done.5, bf16[16,5120]{1,0:T(8,128)(2,1)} %reduce-scatter.3.cloned.1.call-done, f32[1,16,5120]{2,1,0:T(8,128)S(1)} %copy-done.1), kind=kOutput, calls=%fused_computation.46 | convolution fusion | flops 159342080 | bytes 870400 | tf_op jit(solution)/shard_map/dot_general | solution.py:38
  114.8 0.0 copy-start.6
  114.8 3.8 %collective-permute-start.3 = (bf16[16,160]{1,0:T(8,128)(2,1)S(1)}, bf16[16,160]{1,0:T(8,128)(2,1)S(1)}, u32[]{:S(2)}, u32[]{:S(2)}) collective-permute-start(bf16[16,160]{1,0:T(8,128)(2,1)S(1)} %fusion.43), channel_id=1, source_target_pairs={{8,0},{16,8},{24,16},{32,24},{40,32},{48,40},{56,48},{64,56},{72,6... | collective-permute-start | bytes 15368 | tf_op jit(solution)/shard_map/ppermute | solution.py:18
  118.7 1.9 collective-permute-start.1
  120.6 0.0 copy-done.2
  120.6 0.7 clamp_convert_fusion.1
  121.3 7.5 %collective-permute-start.2 = (bf16[16,5120]{1,0:T(8,128)(2,1)S(1)}, bf16[16,5120]{1,0:T(8,128)(2,1)S(1)}, u32[]{:S(2)}, u32[]{:S(2)}) collective-permute-start(bf16[16,5120]{1,0:T(8,128)(2,1)S(1)} %get-tuple-element.10), channel_id=1, source_target_pairs={{8,0},{16,8},{24,16},{32,24},{40,32},{48,40},{56,48},{64,56},{72,6... | collective-permute-start | bytes 491528 | tf_op jit(solution)/shard_map/ppermute | solution.py:18
  128.8 1.9 collective-permute-start
  130.8 0.0 collective-permute-done.1
  130.8 0.6 fusion.5
  131.4 76.9 %reduce-scatter.5.cloned.1.call-done = bf16[16,5120]{1,0:T(8,128)(2,1)} async-done(((bf16[128,5120]{1,0:T(8,128)(2,1)}), bf16[16,5120]{1,0:T(8,128)(2,1)}) %reduce-scatter.5.cloned.1.call-update) | async-done | bytes 163856 | tf_op jit(solution)/shard_map/reduce_scatter | solution.py:70
  208.2 0.0 collective-permute-done.3
  208.2 0.0 collective-permute-done.2
  208.2 0.0 collective-permute-done
  208.3 0.0 copy-done.6
  208.3 1.7 fusion.55
  209.9 1.6 fusion.42
  211.6 3.3 %collective-permute-start.7 = (bf16[16,160]{1,0:T(8,128)(2,1)S(1)}, bf16[16,160]{1,0:T(8,128)(2,1)S(1)}, u32[]{:S(2)}, u32[]{:S(2)}) collective-permute-start(bf16[16,160]{1,0:T(8,128)(2,1)S(1)} %fusion.42), channel_id=1, source_target_pairs={{8,0},{16,8},{24,16},{32,24},{40,32},{48,40},{56,48},{64,56},{72,6... | collective-permute-start | bytes 15368 | tf_op jit(solution)/shard_map/ppermute | solution.py:18
  214.9 1.9 collective-permute-start.5
  216.8 0.6 fusion.2
  217.4 0.8 fusion.47
  218.2 0.0 copy-start.3
  218.3 7.7 %collective-permute-start.6 = (bf16[16,5120]{1,0:T(8,128)(2,1)S(1)}, bf16[16,5120]{1,0:T(8,128)(2,1)S(1)}, u32[]{:S(2)}, u32[]{:S(2)}) collective-permute-start(bf16[16,5120]{1,0:T(8,128)(2,1)S(1)} %get-tuple-element.4), channel_id=1, source_target_pairs={{8,0},{16,8},{24,16},{32,24},{40,32},{48,40},{56,48},{64,56},{72,6... | collective-permute-start | bytes 491528 | tf_op jit(solution)/shard_map/ppermute | solution.py:18
  225.9 1.9 collective-permute-start.4
  227.9 0.0 collective-permute-done.5
  227.9 0.6 fusion.1
  228.5 0.0 collective-permute-done.7
  228.5 0.6 fusion
  229.1 0.0 collective-permute-done.6
  229.1 7.4 %collective-permute-done.4 = bf16[16,5120]{1,0:T(8,128)(2,1)S(1)} collective-permute-done((bf16[16,5120]{1,0:T(8,128)(2,1)S(1)}, bf16[16,5120]{1,0:T(8,128)(2,1)S(1)}, u32[]{:S(2)}, u32[]{:S(2)}) %collective-permute-start.4) | collective-permute-done | bytes 163872 | tf_op jit(solution)/shard_map/ppermute | solution.py:18
  236.5 0.0 copy-done.3
  236.5 1.1 fusion.57
  (2 shorter events, 0.0 us)
Async XLA Ops:
  7.2 3.2 %copy-start = (bf16[1,2,128,5120]{3,2,1,0:T(8,128)(2,1)S(1)}, bf16[1,2,128,5120]{3,2,1,0:T(8,128)(2,1)}, u32[]{:S(2)}) copy-start(bf16[1,2,128,5120]{3,2,1,0:T(8,128)(2,1)} %param.9) | copy-start | bytes 7864324
  7.2 3.2 %copy-start.4 = (bf16[1,2,128,128]{3,2,1,0:T(8,128)(2,1)S(1)}, bf16[1,2,128,128]{3,2,1,0:T(8,128)(2,1)}, u32[]{:S(2)}) copy-start(bf16[1,2,128,128]{3,2,1,0:T(8,128)(2,1)} %param.8) | copy-start | bytes 196612
  7.2 105.0 %reduce-scatter.3.cloned.1.call-start = ((), (), s32[]{:S(2)}) async-start(), calls=%async_computation.2 | async-start | bytes 1474560 | tf_op jit(solution)/shard_map/reduce_scatter | solution.py:70
  10.3 101.9 %copy-start.1 = (f32[1,16,5120]{2,1,0:T(8,128)S(1)}, f32[1,16,5120]{2,1,0:T(8,128)}, u32[]{:S(2)}) copy-start(f32[1,16,5120]{2,1,0:T(8,128)} %param.5) | copy-start | bytes 983044
  10.3 101.9 %copy-start.5 = (f32[1,16,5120]{2,1,0:T(8,128)S(1)}, f32[1,16,5120]{2,1,0:T(8,128)}, u32[]{:S(2)}) copy-start(f32[1,16,5120]{2,1,0:T(8,128)} %param.6) | copy-start | bytes 983044
  10.3 197.9 %reduce-scatter.5.cloned.1.call-start = ((), (), s32[]{:S(2)}) async-start(), calls=%async_computation.3 | async-start | bytes 1474560 | tf_op jit(solution)/shard_map/reduce_scatter | solution.py:70
  112.2 8.4 %copy-start.2 = (bf16[16,5120]{1,0:T(8,128)(2,1)S(1)}, bf16[16,5120]{1,0:T(8,128)(2,1)}, u32[]{:S(2)}) copy-start(bf16[16,5120]{1,0:T(8,128)(2,1)} %reduce-scatter.3.cloned.1.call-done) | copy-start | bytes 491524
  114.8 93.4 %copy-start.6 = (f32[1,16,5120]{2,1,0:T(8,128)S(1)}, f32[1,16,5120]{2,1,0:T(8,128)}, u32[]{:S(2)}) copy-start(f32[1,16,5120]{2,1,0:T(8,128)} %param.7) | copy-start | bytes 983044
  114.8 93.4 %collective-permute-start.3 = (bf16[16,160]{1,0:T(8,128)(2,1)S(1)}, bf16[16,160]{1,0:T(8,128)(2,1)S(1)}, u32[]{:S(2)}, u32[]{:S(2)}) collective-permute-start(bf16[16,160]{1,0:T(8,128)(2,1)S(1)} %fusion.43), channel_id=1, source_target_pairs={{8,0},{16,8},{24,16},{32,24},{40,32},{48,40},{56,48},{64,56},{72,6... | collective-permute-start | bytes 15368 | tf_op jit(solution)/shard_map/ppermute | solution.py:18
  118.7 12.1 %collective-permute-start.1 = (bf16[16,160]{1,0:T(8,128)(2,1)S(1)}, bf16[16,160]{1,0:T(8,128)(2,1)S(1)}, u32[]{:S(2)}, u32[]{:S(2)}) collective-permute-start(bf16[16,160]{1,0:T(8,128)(2,1)S(1)} %fusion.43), channel_id=1, source_target_pairs={{504,0},{0,8},{8,16},{16,24},{24,32},{32,40},{40,48},{48,56},{56,6... | collective-permute-start | bytes 15368 | tf_op jit(solution)/shard_map/ppermute | solution.py:18
  121.3 87.0 %collective-permute-start.2 = (bf16[16,5120]{1,0:T(8,128)(2,1)S(1)}, bf16[16,5120]{1,0:T(8,128)(2,1)S(1)}, u32[]{:S(2)}, u32[]{:S(2)}) collective-permute-start(bf16[16,5120]{1,0:T(8,128)(2,1)S(1)} %get-tuple-element.10), channel_id=1, source_target_pairs={{8,0},{16,8},{24,16},{32,24},{40,32},{48,40},{56,48},{64,56},{72,6... | collective-permute-start | bytes 491528 | tf_op jit(solution)/shard_map/ppermute | solution.py:18
  128.8 79.4 %collective-permute-start = (bf16[16,5120]{1,0:T(8,128)(2,1)S(1)}, bf16[16,5120]{1,0:T(8,128)(2,1)S(1)}, u32[]{:S(2)}, u32[]{:S(2)}) collective-permute-start(bf16[16,5120]{1,0:T(8,128)(2,1)S(1)} %get-tuple-element.10), channel_id=1, source_target_pairs={{504,0},{0,8},{8,16},{16,24},{24,32},{32,40},{40,48},{48,56},{56,6... | collective-permute-start | bytes 491528 | tf_op jit(solution)/shard_map/ppermute | solution.py:18
  211.6 16.9 %collective-permute-start.7 = (bf16[16,160]{1,0:T(8,128)(2,1)S(1)}, bf16[16,160]{1,0:T(8,128)(2,1)S(1)}, u32[]{:S(2)}, u32[]{:S(2)}) collective-permute-start(bf16[16,160]{1,0:T(8,128)(2,1)S(1)} %fusion.42), channel_id=1, source_target_pairs={{8,0},{16,8},{24,16},{32,24},{40,32},{48,40},{56,48},{64,56},{72,6... | collective-permute-start | bytes 15368 | tf_op jit(solution)/shard_map/ppermute | solution.py:18
  214.9 13.0 %collective-permute-start.5 = (bf16[16,160]{1,0:T(8,128)(2,1)S(1)}, bf16[16,160]{1,0:T(8,128)(2,1)S(1)}, u32[]{:S(2)}, u32[]{:S(2)}) collective-permute-start(bf16[16,160]{1,0:T(8,128)(2,1)S(1)} %fusion.42), channel_id=1, source_target_pairs={{504,0},{0,8},{8,16},{16,24},{24,32},{32,40},{40,48},{48,56},{56,6... | collective-permute-start | bytes 15368 | tf_op jit(solution)/shard_map/ppermute | solution.py:18
  218.2 18.2 %copy-start.3 = (bf16[16,5120]{1,0:T(8,128)(2,1)S(1)}, bf16[16,5120]{1,0:T(8,128)(2,1)}, u32[]{:S(2)}) copy-start(bf16[16,5120]{1,0:T(8,128)(2,1)} %reduce-scatter.5.cloned.1.call-done) | copy-start | bytes 491524
  218.3 10.9 %collective-permute-start.6 = (bf16[16,5120]{1,0:T(8,128)(2,1)S(1)}, bf16[16,5120]{1,0:T(8,128)(2,1)S(1)}, u32[]{:S(2)}, u32[]{:S(2)}) collective-permute-start(bf16[16,5120]{1,0:T(8,128)(2,1)S(1)} %get-tuple-element.4), channel_id=1, source_target_pairs={{8,0},{16,8},{24,16},{32,24},{40,32},{48,40},{56,48},{64,56},{72,6... | collective-permute-start | bytes 491528 | tf_op jit(solution)/shard_map/ppermute | solution.py:18
  225.9 10.5 %collective-permute-start.4 = (bf16[16,5120]{1,0:T(8,128)(2,1)S(1)}, bf16[16,5120]{1,0:T(8,128)(2,1)S(1)}, u32[]{:S(2)}, u32[]{:S(2)}) collective-permute-start(bf16[16,5120]{1,0:T(8,128)(2,1)S(1)} %get-tuple-element.4), channel_id=1, source_target_pairs={{504,0},{0,8},{8,16},{16,24},{24,32},{32,40},{40,48},{48,56},{56,6... | collective-permute-start | bytes 491528 | tf_op jit(solution)/shard_map/ppermute | solution.py:18
Sparse Core Ops, SparseCore 0:
  12.6 99.5 reduce-scatter.2
  117.4 90.7 reduce-scatter.4
where the time goes:
time: 245 us; the launch traced here: 244 us
  waiting for transfers between devices  184 us (75%)
  starting transfers between devices  30.1 us (12%)
  between operations  14.2 us (6%)
  matrix products  13.8 us (6%)
    reduce_scatter x2, waiting for transfers between devices, per_device(): lax.psum_scatter(round_term(activations[round_index], cotangents[round_in...  177 us
    ppermute x8, starting transfers between devices, passed_along(): return lax.ppermute(block, axis, route)  30 us
    ppermute x8, waiting for transfers between devices, passed_along(): return lax.ppermute(block, axis, route)  7.38 us
  transfers between devices with their start and end apart: 10, of which 3 were waited for; matrix products, arithmetic and copies ran while one was open for 3% of the time, Pallas kernels for 0%

commit v1 on v0

v1 whole, which is shorter than its diff:
```python
import functools

import jax
import jax.numpy as jnp
from jax import lax
from jax.experimental import pallas as pl
from jax.experimental.pallas import tpu as pltpu
from jax.sharding import PartitionSpec as P

MESH = pl.DeviceIdType.MESH
BLOCK = 32
LANES = 128
LEARN_RATE = 0.25
MIX_RATE = 0.4
SCALE_FLOOR = 0.25
CODE_LIMIT = 2.0
CHUNKS = 5
XSIDE = 4
AHEAD = 3
LAGS = (2, 4, 6)

TO_RIGHT, TO_LEFT, SUM_O, SUM_M, OVER, GO_AFTER, GO_BEFORE = range(7)
PARTS, SUMS, ACROSS, GOSSIP = range(4)
LANDS = ((0, 4), (4, 2), (6, 1), (7, 2))
INBOX = 9
NEAR_M, FAR_O, FAR_M, NEAR_O, IN_SUM_O, IN_SUM_M, IN_ACROSS, IN_BEFORE, IN_AFTER = range(INBOX)

OWN_MINE, NEXT_OTHER, LAST_MINE, OWN_OTHER = 0, 1, 2, 3
LEFT_PAIR, RIGHT_PAIR = 4, 6


def tall(wide):
    n = wide.shape[1] // LANES
    return jnp.concatenate([wide[:, i * LANES:(i + 1) * LANES] for i in range(n)], axis=0)


def flat(high, rows):
    n = high.shape[0] // rows
    return jnp.concatenate([high[i * rows:(i + 1) * rows] for i in range(n)], axis=1)


def add(*refs):
    total = refs[0][...].astype(jnp.float32)
    for ref in refs[1:]:
        total = total + ref[...].astype(jnp.float32)
    return total


def kernel(par_hbm, pub_hbm, mix_hbm, hid_hbm, cot_hbm, opar, opub, omix,
           hid, hid_t, cot, par, pub, mix, part, inbox, fwd_o, fwd_m, zout, gout, step_v, mess_v, pool,
           hid_sem, cot_sem, state_sem, send_sem, recv_sem):
    rounds, tokens, rows_all = hid.shape
    chunks, rows, w = par.shape
    items = rounds * chunks

    b = lax.axis_index("blk")
    f = lax.axis_index("fsdp")
    nb = lax.axis_size("blk")
    x, zh = f // 2, f % 2
    right = (b, (x + 1) % XSIDE * 2 + zh)
    left = (b, (x + XSIDE - 1) % XSIDE * 2 + zh)
    across = (b, x * 2 + 1 - zh)
    after = ((b + 1) % nb, f)
    before = ((b + nb - 1) % nb, f)

    barrier = pltpu.get_barrier_semaphore()
    for device in (right, left, across, after, before):
        pl.semaphore_signal(barrier, inc=1, device_id=device, device_id_type=MESH)

    def cols(c):
        return pl.ds(pl.multiple_of(c * w, LANES), w)

    hid_load = pltpu.make_async_copy(hid_hbm.at[0], hid, hid_sem.at[0])

    def cot_load(t):
        return pltpu.make_async_copy(cot_hbm.at[0, t // chunks, :, cols(t % chunks)], cot.at[t], cot_sem.at[t])

    def state_loads(c):
        return [pltpu.make_async_copy(src.at[0, :, cols(c)], dst.at[c], state_sem.at[i, c])
                for i, (src, dst) in enumerate(((par_hbm, par), (pub_hbm, pub), (mix_hbm, mix)))]

    hid_load.start()
    for t in range(AHEAD):
        cot_load(t).start()

    @pl.loop(AHEAD, items)
    def _(t):
        cot_load(t).start()

    @pl.loop(0, chunks)
    def _(c):
        for copy in state_loads(c):
            copy.start()

    def land(t, first, blocks=1):
        return inbox.at[t, pl.ds(first, blocks)]

    def start(kind, t):
        src, dst, device, group = {
            TO_RIGHT: lambda: (part.at[t, pl.ds(RIGHT_PAIR, 2)], land(t, NEAR_M, 2), right, PARTS),
            TO_LEFT: lambda: (part.at[t, pl.ds(LEFT_PAIR, 2)], land(t, FAR_M, 2), left, PARTS),
            SUM_O: lambda: (fwd_o.at[pl.ds(t, 1)], land(t, IN_SUM_O), right, SUMS),
            SUM_M: lambda: (fwd_m.at[pl.ds(t, 1)], land(t, IN_SUM_M), left, SUMS),
            OVER: lambda: (zout.at[pl.ds(t, 1)], land(t, IN_ACROSS), across, ACROSS),
            GO_AFTER: lambda: (gout.at[pl.ds(t, 1)], land(t, IN_BEFORE), after, GOSSIP),
            GO_BEFORE: lambda: (gout.at[pl.ds(t, 1)], land(t, IN_AFTER), before, GOSSIP),
        }[kind]()
        pltpu.make_async_remote_copy(
            src_ref=src, dst_ref=dst, send_sem=send_sem.at[0], recv_sem=recv_sem.at[group, t],
            device_id=device, device_id_type=MESH).start()

    def arrived(group, t):
        blocks = land(t, *LANDS[group])
        pltpu.make_async_copy(blocks, blocks, recv_sem.at[group, t]).wait()

    places = [3 * ((j // 2 + XSIDE - x) % XSIDE * 2 + (j + zh) % 2) % 8 for j in range(rows_all // rows)]

    def multiply(t):
        cot_load(t).wait()
        product = jnp.dot(hid_t[t // chunks], cot[t], preferred_element_type=jnp.float32).astype(jnp.bfloat16)
        for j, place in enumerate(places):
            part[t, place] = product[j * rows:(j + 1) * rows]

    def send_parts(t):
        start(TO_RIGHT, t)
        start(TO_LEFT, t)

    def pass_on(t):
        arrived(PARTS, t)
        fwd_o[t] = add(inbox.at[t, FAR_O], part.at[t, NEXT_OTHER]).astype(jnp.bfloat16)
        start(SUM_O, t)
        fwd_m[t] = add(inbox.at[t, FAR_M], part.at[t, LAST_MINE]).astype(jnp.bfloat16)
        start(SUM_M, t)

    def over_z(t):
        arrived(SUMS, t)
        zout[t] = add(part.at[t, OWN_OTHER], inbox.at[t, NEAR_O], inbox.at[t, IN_SUM_O]).astype(jnp.bfloat16)
        start(OVER, t)

    def encode(t):
        c = t % chunks

        @pl.when(t < chunks)
        def _():
            for copy in state_loads(c):
                copy.wait()

        arrived(ACROSS, t)
        gradient = add(part.at[t, OWN_MINE], inbox.at[t, NEAR_M], inbox.at[t, IN_SUM_M], inbox.at[t, IN_ACROSS])
        stepped = par[c] - LEARN_RATE * gradient
        public = pub[c]
        change = tall(stepped - public)
        square = change * change
        high = square.astype(jnp.bfloat16)
        low = (square - high.astype(jnp.float32)).astype(jnp.bfloat16)
        energy = jnp.dot(jnp.concatenate([high, low], axis=1), pool[...], preferred_element_type=jnp.float32)
        scales = jnp.maximum(jnp.sqrt(energy * (1.0 / BLOCK)), SCALE_FLOOR).astype(jnp.bfloat16)
        wide = scales.astype(jnp.float32)
        coded = jnp.clip(change / wide, -CODE_LIMIT, CODE_LIMIT).astype(jnp.bfloat16)
        message = flat(coded.astype(jnp.float32) * wide, rows)
        gout[t] = message.astype(jnp.bfloat16)
        start(GO_AFTER, t)
        start(GO_BEFORE, t)
        pub[c] = public + message
        step_v[c] = stepped
        mess_v[c] = message

    def update(t):
        c = t % chunks
        arrived(GOSSIP, t)
        public = pub[c]
        heard = mess_v[c] + add(inbox.at[t, IN_BEFORE], inbox.at[t, IN_AFTER])
        mixed = mix[c] + heard * (1.0 / 3.0)
        params = step_v[c] + MIX_RATE * (mixed - public)

        @pl.when(t < items - chunks)
        def _():
            mix[c] = mixed
            par[c] = params

        @pl.when(t >= items - chunks)
        def _():
            opar[0, :, cols(c)] = params
            opub[0, :, cols(c)] = public
            omix[0, :, cols(c)] = mixed

    block = lax.broadcasted_iota(jnp.int32, pool.shape, 0) % LANES // BLOCK
    lane_block = lax.broadcasted_iota(jnp.int32, pool.shape, 1) // BLOCK

    hid_load.wait()
    hid_t[0] = hid[0].T
    multiply(0)
    pl.semaphore_wait(barrier, 5)
    send_parts(0)
    for t in range(1, AHEAD):
        multiply(t)
        send_parts(t)
    for r in range(1, rounds):
        hid_t[r] = hid[r].T
    pool[...] = (block == lane_block).astype(jnp.bfloat16)

    @pl.loop(AHEAD, items)
    def _(t):
        multiply(t)

    def stage(work, item):
        @pl.when((item >= 0) & (item < items))
        def _():
            work(item)

    @pl.loop(0, items + LAGS[-1])
    def _(t):
        stage(pass_on, t)
        stage(send_parts, t + AHEAD)
        for work, lag in zip((over_z, encode, update), LAGS):
            stage(work, t - lag)

    pltpu.make_async_copy(inbox, inbox, send_sem.at[0]).wait()


def deliver(*refs):
    sem = refs[-1]
    arrays = (len(refs) - 1) // 2
    copies = []
    for i in range(arrays):
        half = refs[i].shape[1] // 2
        for j in range(2):
            piece = (0, pl.ds(j * half, half))
            copies.append(pltpu.make_async_copy(refs[i].at[piece], refs[arrays + i].at[piece], sem.at[i, j]))
    for copy in copies:
        copy.start()
    for copy in copies:
        copy.wait()


def per_device(params, public, mixed, hidden, cotangent):
    _, rows, width = params.shape
    _, rounds, tokens, rows_all = hidden.shape
    items = rounds * CHUNKS
    w = width // CHUNKS
    piece = pltpu.VMEM((items, rows, w), jnp.bfloat16)
    state = pltpu.VMEM((CHUNKS, rows, w), jnp.float32)
    anywhere = pl.BlockSpec(memory_space=pl.ANY)
    in_vmem = pl.BlockSpec(memory_space=pltpu.VMEM)
    results = pl.pallas_call(
        kernel,
        out_shape=(pltpu.VMEM(params.shape, jnp.float32),) * 3,
        in_specs=[anywhere] * 5,
        out_specs=(in_vmem,) * 3,
        scratch_shapes=[
            pltpu.VMEM((rounds, tokens, rows_all), jnp.bfloat16),
            pltpu.VMEM((rounds, rows_all, tokens), jnp.bfloat16),
            pltpu.VMEM((items, tokens, w), jnp.bfloat16),
            state, state, state,
            pltpu.VMEM((items, rows_all // rows, rows, w), jnp.bfloat16),
            pltpu.VMEM((items, INBOX, rows, w), jnp.bfloat16),
            *[piece] * 4,
            state, state,
            pltpu.VMEM((2 * LANES, LANES), jnp.bfloat16),
            pltpu.SemaphoreType.DMA((1,)),
            pltpu.SemaphoreType.DMA((items,)),
            pltpu.SemaphoreType.DMA((3, CHUNKS)),
            pltpu.SemaphoreType.DMA((1,)),
            pltpu.SemaphoreType.DMA((len(LANDS), items)),
        ],
        compiler_params=pltpu.CompilerParams(
            collective_id=0, has_side_effects=True, vmem_limit_bytes=40 * 1024 * 1024),
        cost_estimate=pl.CostEstimate(flops=340_000_000, bytes_accessed=5_000_000, transcendentals=0),
    )(*[pltpu.with_memory_space_constraint(a, pltpu.HBM) for a in (params, public, mixed, hidden, cotangent)])
    return pl.pallas_call(
        deliver,
        out_shape=(jax.ShapeDtypeStruct(params.shape, jnp.float32),) * 3,
        in_specs=[in_vmem] * 3,
        out_specs=(anywhere,) * 3,
        scratch_shapes=[pltpu.SemaphoreType.DMA((3, 2))],
        compiler_params=pltpu.CompilerParams(vmem_limit_bytes=1024 * 1024),
    )(*[pltpu.with_memory_space_constraint(a, pltpu.VMEM) for a in results])


def solution(mesh):
    state = P("blk", "fsdp", None)
    tokens = P("blk", None, "fsdp", None)
    return jax.shard_map(
        per_device,
        mesh=mesh,
        in_specs=(state, state, state, tokens, tokens),
        out_specs=(state, state, state),
        check_vma=False,
    )
```

time: 245 us -> 51.2 us (0.21)
  waiting for transfers between devices: 184 us -> 0 us
  Pallas kernels: 0 us -> 50.2 us
  starting transfers between devices: 30.1 us -> 0 us
  matrix products: 13.8 us -> 0 us
  between operations: 14.2 us -> 0.64 us
    reduce_scatter x2 -> x0, waiting for transfers between devices: 177 us -> none  [per_device(): lax.psum_scatter(round_term(activations[round_index], cotangents[round_in...]
    pallas_call x0 -> x2, Pallas kernels: none -> 50.2 us  [the longest x1 49.3 us: per_device(): pl.pallas_call(kernel, out_shape=(pltpu.VMEM(params.shape, jnp.float32),)...]
    ppermute x8 -> x0, starting transfers between devices: 30 us -> none  [passed_along(): return lax.ppermute(block, axis, route)]
    dot_general x10 -> x0, matrix products: 13.8 us -> none  [the longest x6 4.81 us: spread_out(): lax.dot_general(scales.astype(jnp.float32), pooling, (((1,), (1,)), ((),...]
    ppermute x8 -> x0, waiting for transfers between devices: 7.38 us -> none  [passed_along(): return lax.ppermute(block, axis, route)]
  transfers between devices with their start and end apart: 10 -> 0, of which waited for: 3 -> 0; matrix products, arithmetic and copies ran while one was open for 3% -> 0% of each run, Pallas kernels for 0% -> 0%
where the time goes in v1:
time: 51.2 us; the launch traced here: 50.9 us
  Pallas kernels  50.2 us (98%)
  between operations  0.64 us (1%)
    pallas_call x1, Pallas kernels, per_device(): pl.pallas_call(kernel, out_shape=(pltpu.VMEM(params.shape, jnp.float32),)...  49.3 us

profile of v1, /device:TPU:6, one launch (start us, length us, event | category | flops | bytes accessed | tf_op | source)
XLA Modules:
  0.0 50.9 jit_solution(16927578300030514777)
XLA Ops:
  0.6 49.3 %shard_map.76 = (f32[1,16,5120]{2,1,0:T(8,128)S(1)}, f32[1,16,5120]{2,1,0:T(8,128)S(1)}, f32[1,16,5120]{2,1,0:T(8,128)S(1)}) custom-call(f32[1,16,5120]{2,1,0:T(8,128)} %par_hbm.1, f32[1,16,5120]{2,1,0:T(8,128)} %pub_hbm.1, f32[1,16,5120]{2,1,0:T(8,128)} %mix_hbm.1, bf16[1,2,128,128]{3,2,1,0:T(8,128)(2,1)} %hid_hbm.1, bf16[1,2,128,5120]{3,2,1,0:T(8,128)(2,1)} %cot_hbm.1), custom_call_target="tpu_custom_call" | custom-call | flops 340000000 | bytes 5000000 | tf_op jit(solution)/shard_map/pallas_call | solution.py:245
  49.9 1.0 %shard_map.77 = (f32[1,16,5120]{2,1,0:T(8,128)}, f32[1,16,5120]{2,1,0:T(8,128)}, f32[1,16,5120]{2,1,0:T(8,128)}) custom-call(f32[1,16,5120]{2,1,0:T(8,128)S(1)} %get-tuple-element.6.refs_0_, f32[1,16,5120]{2,1,0:T(8,128)S(1)} %get-tuple-element.7.refs_1_, f32[1,16,5120]{2,1,0:T(8,128)S(1)} %get-tuple-element.8.refs_2_), custom_call_target="tpu_custom_call" | custom-call | tf_op jit(solution)/shard_map/pallas_call | solution.py:270

commit v2 on v1

--- a/solution.py
+++ b/solution.py
@@ -25,6 +25,9 @@
 INBOX = 9
 NEAR_M, FAR_O, FAR_M, NEAR_O, IN_SUM_O, IN_SUM_M, IN_ACROSS, IN_BEFORE, IN_AFTER = range(INBOX)
 
+PIECES = 2
+LANDS_LAST = {PARTS: (0, 6), ACROSS: (6, 1), GOSSIP: (7, 2)}
+
 OWN_MINE, NEXT_OTHER, LAST_MINE, OWN_OTHER = 0, 1, 2, 3
 LEFT_PAIR, RIGHT_PAIR = 4, 6
 
@@ -48,10 +51,12 @@
 
 def kernel(par_hbm, pub_hbm, mix_hbm, hid_hbm, cot_hbm, opar, opub, omix,
            hid, hid_t, cot, par, pub, mix, part, inbox, fwd_o, fwd_m, zout, gout, step_v, mess_v, pool,
-           hid_sem, cot_sem, state_sem, send_sem, recv_sem):
+           last_part, last_inbox, last_zout, last_gout,
+           hid_sem, cot_sem, state_sem, send_sem, recv_sem, last_recv_sem):
     rounds, tokens, rows_all = hid.shape
     chunks, rows, w = par.shape
-    items = rounds * chunks
+    items = rounds * chunks - 1
+    wl = w // PIECES
 
     b = lax.axis_index("blk")
     f = lax.axis_index("fsdp")
@@ -60,11 +65,12 @@
     right = (b, (x + 1) % XSIDE * 2 + zh)
     left = (b, (x + XSIDE - 1) % XSIDE * 2 + zh)
     across = (b, x * 2 + 1 - zh)
+    opposite = (b, (x + 2) % XSIDE * 2 + zh)
     after = ((b + 1) % nb, f)
     before = ((b + nb - 1) % nb, f)
 
     barrier = pltpu.get_barrier_semaphore()
-    for device in (right, left, across, after, before):
+    for device in (right, left, opposite, across, after, before):
         pl.semaphore_signal(barrier, inc=1, device_id=device, device_id_type=MESH)
 
     def cols(c):
@@ -82,15 +88,6 @@
     hid_load.start()
     for t in range(AHEAD):
         cot_load(t).start()
-
-    @pl.loop(AHEAD, items)
-    def _(t):
-        cot_load(t).start()
-
-    @pl.loop(0, chunks)
-    def _(c):
-        for copy in state_loads(c):
-            copy.start()
 
     def land(t, first, blocks=1):
         return inbox.at[t, pl.ds(first, blocks)]
@@ -115,11 +112,20 @@
 
     places = [3 * ((j // 2 + XSIDE - x) % XSIDE * 2 + (j + zh) % 2) % 8 for j in range(rows_all // rows)]
 
+    def product(t):
+        cot_load(t).wait()
+        return jnp.dot(hid_t[t // chunks], cot[t], preferred_element_type=jnp.float32).astype(jnp.bfloat16)
+
     def multiply(t):
-        cot_load(t).wait()
-        product = jnp.dot(hid_t[t // chunks], cot[t], preferred_element_type=jnp.float32).astype(jnp.bfloat16)
+        blocks = product(t)
         for j, place in enumerate(places):
-            part[t, place] = product[j * rows:(j + 1) * rows]
+            part[t, place] = blocks[j * rows:(j + 1) * rows]
+
+    def multiply_last():
+        blocks = product(items)
+        for j, place in enumerate(places):
+            for k in range(PIECES):
+                last_part[k, place * 3 % 8] = blocks[j * rows:(j + 1) * rows, k * wl:(k + 1) * wl]
 
     def send_parts(t):
         start(TO_RIGHT, t)
@@ -137,18 +143,9 @@
         zout[t] = add(part.at[t, OWN_OTHER], inbox.at[t, NEAR_O], inbox.at[t, IN_SUM_O]).astype(jnp.bfloat16)
         start(OVER, t)
 
-    def encode(t):
-        c = t % chunks
-
-        @pl.when(t < chunks)
-        def _():
-            for copy in state_loads(c):
-                copy.wait()
-
-        arrived(ACROSS, t)
-        gradient = add(part.at[t, OWN_MINE], inbox.at[t, NEAR_M], inbox.at[t, IN_SUM_M], inbox.at[t, IN_ACROSS])
-        stepped = par[c] - LEARN_RATE * gradient
-        public = pub[c]
+    def code(c, columns, gradient):
+        stepped = par[c, :, columns] - LEARN_RATE * gradient
+        public = pub[c, :, columns]
         change = tall(stepped - public)
         square = change * change
         high = square.astype(jnp.bfloat16)
@@ -158,40 +155,101 @@
         wide = scales.astype(jnp.float32)
         coded = jnp.clip(change / wide, -CODE_LIMIT, CODE_LIMIT).astype(jnp.bfloat16)
         message = flat(coded.astype(jnp.float32) * wide, rows)
-        gout[t] = message.astype(jnp.bfloat16)
+        pub[c, :, columns] = public + message
+        step_v[c, :, columns] = stepped
+        mess_v[c, :, columns] = message
+        return message.astype(jnp.bfloat16)
+
+    def mix_in(c, columns, heard):
+        public = pub[c, :, columns]
+        mixed = mix[c, :, columns] + (mess_v[c, :, columns] + heard) * (1.0 / 3.0)
+        return step_v[c, :, columns] + MIX_RATE * (mixed - public), public, mixed
+
+    def encode(t):
+        c = t % chunks
+
+        @pl.when(t < chunks)
+        def _():
+            for copy in state_loads(c):
+                copy.wait()
+
+        arrived(ACROSS, t)
+        gradient = add(part.at[t, OWN_MINE], inbox.at[t, NEAR_M], inbox.at[t, IN_SUM_M], inbox.at[t, IN_ACROSS])
+        gout[t] = code(c, slice(0, w), gradient)
         start(GO_AFTER, t)
         start(GO_BEFORE, t)
-        pub[c] = public + message
-        step_v[c] = stepped
-        mess_v[c] = message
 
     def update(t):
         c = t % chunks
         arrived(GOSSIP, t)
-        public = pub[c]
-        heard = mess_v[c] + add(inbox.at[t, IN_BEFORE], inbox.at[t, IN_AFTER])
-        mixed = mix[c] + heard * (1.0 / 3.0)
-        params = step_v[c] + MIX_RATE * (mixed - public)
-
-        @pl.when(t < items - chunks)
+        params, public, mixed = mix_in(c, slice(0, w), add(inbox.at[t, IN_BEFORE], inbox.at[t, IN_AFTER]))
+
+        @pl.when(t < (rounds - 1) * chunks)
         def _():
             mix[c] = mixed
             par[c] = params
 
-        @pl.when(t >= items - chunks)
+        @pl.when(t >= (rounds - 1) * chunks)
         def _():
             opar[0, :, cols(c)] = params
             opub[0, :, cols(c)] = public
             omix[0, :, cols(c)] = mixed
 
+    def last_start(k, src, slot, device, group):
+        pltpu.make_async_remote_copy(
+            src_ref=src, dst_ref=last_inbox.at[k, pl.ds(slot, src.shape[0])], send_sem=send_sem.at[1],
+            recv_sem=last_recv_sem.at[group, k], device_id=device, device_id_type=MESH).start()
+
+    def last_arrived(group, k):
+        first, blocks = LANDS_LAST[group]
+        blocks = last_inbox.at[k, pl.ds(first, blocks)]
+        pltpu.make_async_copy(blocks, blocks, last_recv_sem.at[group, k]).wait()
+
+    def last_send_parts(k):
+        for d, device in ((2, opposite), (1, right), (3, left)):
+            last_start(k, last_part.at[k, pl.ds(2 * d, 2)], 2 * d - 2, device, PARTS)
+
+    def last_over_z(k):
+        last_arrived(PARTS, k)
+        last_zout[k] = add(*[last_part.at[k, 1]] + [last_inbox.at[k, i] for i in (1, 3, 5)]).astype(jnp.bfloat16)
+        last_start(k, last_zout.at[pl.ds(k, 1)], LANDS_LAST[ACROSS][0], across, ACROSS)
+
+    def last_encode(k):
+        last_arrived(ACROSS, k)
+        gradient = add(*[last_part.at[k, 0]] + [last_inbox.at[k, i] for i in (0, 2, 4, 6)])
+        last_gout[k] = code(chunks - 1, slice(k * wl, (k + 1) * wl), gradient)
+        first = LANDS_LAST[GOSSIP][0]
+        last_start(k, last_gout.at[pl.ds(k, 1)], first, after, GOSSIP)
+        last_start(k, last_gout.at[pl.ds(k, 1)], first + 1, before, GOSSIP)
+
+    def last_update(k):
+        last_arrived(GOSSIP, k)
+        columns = slice(k * wl, (k + 1) * wl)
+        first = LANDS_LAST[GOSSIP][0]
+        params, public, mixed = mix_in(chunks - 1, columns, add(last_inbox.at[k, first], last_inbox.at[k, first + 1]))
+        there = pl.ds((chunks - 1) * w + k * wl, wl)
+        opar[0, :, there] = params
+        opub[0, :, there] = public
+        omix[0, :, there] = mixed
+
     block = lax.broadcasted_iota(jnp.int32, pool.shape, 0) % LANES // BLOCK
     lane_block = lax.broadcasted_iota(jnp.int32, pool.shape, 1) // BLOCK
 
     hid_load.wait()
     hid_t[0] = hid[0].T
     multiply(0)
-    pl.semaphore_wait(barrier, 5)
+    pl.semaphore_wait(barrier, 6)
     send_parts(0)
+
+    @pl.loop(AHEAD, items + 1)
+    def _(t):
+        cot_load(t).start()
+
+    @pl.loop(0, chunks)
+    def _(c):
+        for copy in state_loads(c):
+            copy.start()
+
     for t in range(1, AHEAD):
         multiply(t)
         send_parts(t)
@@ -203,10 +261,17 @@
     def _(t):
         multiply(t)
 
+    multiply_last()
+
     def stage(work, item):
         @pl.when((item >= 0) & (item < items))
         def _():
             work(item)
+
+    late = {items - 2: ((last_send_parts, 0),), items - 1: ((last_send_parts, 1),),
+            items: ((last_over_z, 0),), items + 1: ((last_over_z, 1),),
+            items + 2: ((last_encode, 0),), items + 3: ((last_encode, 1),),
+            items + 5: ((last_update, 0), (last_update, 1))}
 
     @pl.loop(0, items + LAGS[-1])
     def _(t):
@@ -214,8 +279,14 @@
         stage(send_parts, t + AHEAD)
         for work, lag in zip((over_z, encode, update), LAGS):
             stage(work, t - lag)
+        for step, works in late.items():
+            @pl.when(t == step)
+            def _():
+                for work, k in works:
+                    work(k)
 
     pltpu.make_async_copy(inbox, inbox, send_sem.at[0]).wait()
+    pltpu.make_async_copy(last_inbox, last_inbox, send_sem.at[1]).wait()
 
 
 def deliver(*refs):
@@ -236,7 +307,7 @@
 def per_device(params, public, mixed, hidden, cotangent):
     _, rows, width = params.shape
     _, rounds, tokens, rows_all = hidden.shape
-    items = rounds * CHUNKS
+    items = rounds * CHUNKS - 1
     w = width // CHUNKS
     piece = pltpu.VMEM((items, rows, w), jnp.bfloat16)
     state = pltpu.VMEM((CHUNKS, rows, w), jnp.float32)
@@ -250,18 +321,23 @@
         scratch_shapes=[
             pltpu.VMEM((rounds, tokens, rows_all), jnp.bfloat16),
             pltpu.VMEM((rounds, rows_all, tokens), jnp.bfloat16),
-            pltpu.VMEM((items, tokens, w), jnp.bfloat16),
+            pltpu.VMEM((items + 1, tokens, w), jnp.bfloat16),
             state, state, state,
             pltpu.VMEM((items, rows_all // rows, rows, w), jnp.bfloat16),
             pltpu.VMEM((items, INBOX, rows, w), jnp.bfloat16),
             *[piece] * 4,
             state, state,
             pltpu.VMEM((2 * LANES, LANES), jnp.bfloat16),
+            pltpu.VMEM((PIECES, rows_all // rows, rows, w // PIECES), jnp.bfloat16),
+            pltpu.VMEM((PIECES, INBOX, rows, w // PIECES), jnp.bfloat16),
+            pltpu.VMEM((PIECES, rows, w // PIECES), jnp.bfloat16),
+            pltpu.VMEM((PIECES, rows, w // PIECES), jnp.bfloat16),
             pltpu.SemaphoreType.DMA((1,)),
-            pltpu.SemaphoreType.DMA((items,)),
+            pltpu.SemaphoreType.DMA((items + 1,)),
             pltpu.SemaphoreType.DMA((3, CHUNKS)),
-            pltpu.SemaphoreType.DMA((1,)),
+            pltpu.SemaphoreType.DMA((2,)),
             pltpu.SemaphoreType.DMA((len(LANDS), items)),
+            pltpu.SemaphoreType.DMA((len(LANDS), PIECES)),
         ],
         compiler_params=pltpu.CompilerParams(
             collective_id=0, has_side_effects=True, vmem_limit_bytes=40 * 1024 * 1024),

time: 51.2 us -> 50.8 us (level)
  Pallas kernels: 50.2 us -> 49.4 us
    pallas_call x1, Pallas kernels: 49.3 us -> 48.4 us  [per_device(): pl.pallas_call(kernel, out_shape=(pltpu.VMEM(params.shape, jnp.float32),)...]
where the time goes in v2:
time: 50.8 us; the launch traced here: 50.1 us
  Pallas kernels  49.4 us (97%)
  between operations  0.64 us (1%)
    pallas_call x1, Pallas kernels, per_device(): pl.pallas_call(kernel, out_shape=(pltpu.VMEM(params.shape, jnp.float32),)...  48.4 us

profile of v2, /device:TPU:6, one launch (start us, length us, event | category | flops | bytes accessed | tf_op | source)
XLA Modules:
  0.0 50.1 jit_solution(8488418023776365492)
XLA Ops:
  0.6 48.4 %shard_map.76 = (f32[1,16,5120]{2,1,0:T(8,128)S(1)}, f32[1,16,5120]{2,1,0:T(8,128)S(1)}, f32[1,16,5120]{2,1,0:T(8,128)S(1)}) custom-call(f32[1,16,5120]{2,1,0:T(8,128)} %par_hbm.1, f32[1,16,5120]{2,1,0:T(8,128)} %pub_hbm.1, f32[1,16,5120]{2,1,0:T(8,128)} %mix_hbm.1, bf16[1,2,128,128]{3,2,1,0:T(8,128)(2,1)} %hid_hbm.1, bf16[1,2,128,5120]{3,2,1,0:T(8,128)(2,1)} %cot_hbm.1), custom_call_target="tpu_custom_call" | custom-call | flops 340000000 | bytes 5000000 | tf_op jit(solution)/shard_map/pallas_call | solution.py:316
  49.1 1.0 %shard_map.77 = (f32[1,16,5120]{2,1,0:T(8,128)}, f32[1,16,5120]{2,1,0:T(8,128)}, f32[1,16,5120]{2,1,0:T(8,128)}) custom-call(f32[1,16,5120]{2,1,0:T(8,128)S(1)} %get-tuple-element.6.refs_0_, f32[1,16,5120]{2,1,0:T(8,128)S(1)} %get-tuple-element.7.refs_1_, f32[1,16,5120]{2,1,0:T(8,128)S(1)} %get-tuple-element.8.refs_2_), custom_call_target="tpu_custom_call" | custom-call | tf_op jit(solution)/shard_map/pallas_call | solution.py:346

commit v3 on v2

--- a/solution.py
+++ b/solution.py
@@ -14,7 +14,7 @@
 MIX_RATE = 0.4
 SCALE_FLOOR = 0.25
 CODE_LIMIT = 2.0
-CHUNKS = 5
+CHUNKS = 4
 XSIDE = 4
 AHEAD = 3
 LAGS = (2, 4, 6)
@@ -25,8 +25,9 @@
 INBOX = 9
 NEAR_M, FAR_O, FAR_M, NEAR_O, IN_SUM_O, IN_SUM_M, IN_ACROSS, IN_BEFORE, IN_AFTER = range(INBOX)
 
-PIECES = 2
-LANDS_LAST = {PARTS: (0, 6), ACROSS: (6, 1), GOSSIP: (7, 2)}
+PIECES = 4
+LANDS_X_FIRST = {PARTS: (0, 6), ACROSS: (6, 1), GOSSIP: (7, 2)}
+LANDS_Z_FIRST = {ACROSS: (0, 4), PARTS: (4, 3), GOSSIP: (7, 2)}
 
 OWN_MINE, NEXT_OTHER, LAST_MINE, OWN_OTHER = 0, 1, 2, 3
 LEFT_PAIR, RIGHT_PAIR = 4, 6
@@ -51,12 +52,12 @@
 
 def kernel(par_hbm, pub_hbm, mix_hbm, hid_hbm, cot_hbm, opar, opub, omix,
            hid, hid_t, cot, par, pub, mix, part, inbox, fwd_o, fwd_m, zout, gout, step_v, mess_v, pool,
-           last_part, last_inbox, last_zout, last_gout,
+           last_part, last_inbox, last_zout, last_sums, last_gout,
            hid_sem, cot_sem, state_sem, send_sem, recv_sem, last_recv_sem):
     rounds, tokens, rows_all = hid.shape
     chunks, rows, w = par.shape
-    items = rounds * chunks - 1
-    wl = w // PIECES
+    items = rounds * chunks - 2
+    wl = w // 2
 
     b = lax.axis_index("blk")
     f = lax.axis_index("fsdp")
@@ -121,11 +122,14 @@
         for j, place in enumerate(places):
             part[t, place] = blocks[j * rows:(j + 1) * rows]
 
-    def multiply_last():
-        blocks = product(items)
+    def multiply_last(pair):
+        blocks = product(items + pair)
         for j, place in enumerate(places):
-            for k in range(PIECES):
-                last_part[k, place * 3 % 8] = blocks[j * rows:(j + 1) * rows, k * wl:(k + 1) * wl]
+            which = place * 3 % 8
+            if pair == 1:
+                which = which % 2 * XSIDE + which // 2
+            for i in range(2):
+                last_part[2 * pair + i, which] = blocks[j * rows:(j + 1) * rows, i * wl:(i + 1) * wl]
 
     def send_parts(t):
         start(TO_RIGHT, t)
@@ -195,39 +199,57 @@
             opub[0, :, cols(c)] = public
             omix[0, :, cols(c)] = mixed
 
+    def lands(group, k):
+        return (LANDS_X_FIRST if k < 2 else LANDS_Z_FIRST)[group]
+
+    def place_of(k):
+        return chunks - 2 + k // 2, slice(k % 2 * wl, k % 2 * wl + wl)
+
     def last_start(k, src, slot, device, group):
         pltpu.make_async_remote_copy(
             src_ref=src, dst_ref=last_inbox.at[k, pl.ds(slot, src.shape[0])], send_sem=send_sem.at[1],
             recv_sem=last_recv_sem.at[group, k], device_id=device, device_id_type=MESH).start()
 
     def last_arrived(group, k):
-        first, blocks = LANDS_LAST[group]
+        first, blocks = lands(group, k)
         blocks = last_inbox.at[k, pl.ds(first, blocks)]
         pltpu.make_async_copy(blocks, blocks, last_recv_sem.at[group, k]).wait()
 
+    beyond = ((2, opposite), (1, right), (3, left))
+
     def last_send_parts(k):
-        for d, device in ((2, opposite), (1, right), (3, left)):
+        for d, device in beyond:
             last_start(k, last_part.at[k, pl.ds(2 * d, 2)], 2 * d - 2, device, PARTS)
 
     def last_over_z(k):
         last_arrived(PARTS, k)
         last_zout[k] = add(*[last_part.at[k, 1]] + [last_inbox.at[k, i] for i in (1, 3, 5)]).astype(jnp.bfloat16)
-        last_start(k, last_zout.at[pl.ds(k, 1)], LANDS_LAST[ACROSS][0], across, ACROSS)
+        last_start(k, last_zout.at[pl.ds(k, 1)], lands(ACROSS, k)[0], across, ACROSS)
+
+    def early_over_z(k):
+        last_start(k, last_part.at[k, pl.ds(XSIDE, XSIDE)], 0, across, ACROSS)
+
+    def late_send_parts(k):
+        last_arrived(ACROSS, k)
+        for d, device in beyond:
+            last_sums[k - 2, d - 1] = add(last_part.at[k, d], last_inbox.at[k, d]).astype(jnp.bfloat16)
+            last_start(k, last_sums.at[k - 2, pl.ds(d - 1, 1)], lands(PARTS, k)[0] + d - 1, device, PARTS)
 
     def last_encode(k):
-        last_arrived(ACROSS, k)
-        gradient = add(*[last_part.at[k, 0]] + [last_inbox.at[k, i] for i in (0, 2, 4, 6)])
-        last_gout[k] = code(chunks - 1, slice(k * wl, (k + 1) * wl), gradient)
-        first = LANDS_LAST[GOSSIP][0]
+        last_arrived(ACROSS if k < 2 else PARTS, k)
+        gradient = add(*[last_part.at[k, 0]] + [last_inbox.at[k, i] for i in ((0, 2, 4, 6) if k < 2 else (0, 4, 5, 6))])
+        c, columns = place_of(k)
+        last_gout[k] = code(c, columns, gradient)
+        first = lands(GOSSIP, k)[0]
         last_start(k, last_gout.at[pl.ds(k, 1)], first, after, GOSSIP)
         last_start(k, last_gout.at[pl.ds(k, 1)], first + 1, before, GOSSIP)
 
     def last_update(k):
         last_arrived(GOSSIP, k)
-        columns = slice(k * wl, (k + 1) * wl)
-        first = LANDS_LAST[GOSSIP][0]
-        params, public, mixed = mix_in(chunks - 1, columns, add(last_inbox.at[k, first], last_inbox.at[k, first + 1]))
-        there = pl.ds((chunks - 1) * w + k * wl, wl)
+        c, columns = place_of(k)
+        first = lands(GOSSIP, k)[0]
+        params, public, mixed = mix_in(c, columns, add(last_inbox.at[k, first], last_inbox.at[k, first + 1]))
+        there = pl.ds(c * w + columns.start, wl)
         opar[0, :, there] = params
         opub[0, :, there] = public
         omix[0, :, there] = mixed
@@ -241,7 +263,7 @@
     pl.semaphore_wait(barrier, 6)
     send_parts(0)
 
-    @pl.loop(AHEAD, items + 1)
+    @pl.loop(AHEAD, items + 2)
     def _(t):
         cot_load(t).start()
 
@@ -257,33 +279,39 @@
         hid_t[r] = hid[r].T
     pool[...] = (block == lane_block).astype(jnp.bfloat16)
 
+    multiply_last(1)
+    early_over_z(2)
+    early_over_z(3)
+
     @pl.loop(AHEAD, items)
     def _(t):
         multiply(t)
 
-    multiply_last()
+    multiply_last(0)
 
     def stage(work, item):
         @pl.when((item >= 0) & (item < items))
         def _():
             work(item)
 
-    late = {items - 2: ((last_send_parts, 0),), items - 1: ((last_send_parts, 1),),
+    late = {items - 3: ((last_send_parts, 0),), items - 2: ((last_send_parts, 1),),
+            items - 1: ((late_send_parts, 2), (late_send_parts, 3)),
             items: ((last_over_z, 0),), items + 1: ((last_over_z, 1),),
-            items + 2: ((last_encode, 0),), items + 3: ((last_encode, 1),),
-            items + 5: ((last_update, 0), (last_update, 1))}
+            items + 3: ((last_encode, 0), (last_encode, 2), (last_encode, 3)), items + 4: ((last_encode, 1),),
+            items + 5: ((last_update, 0), (last_update, 2), (last_update, 3), (last_update, 1))}
 
     @pl.loop(0, items + LAGS[-1])
     def _(t):
         stage(pass_on, t)
         stage(send_parts, t + AHEAD)
-        for work, lag in zip((over_z, encode, update), LAGS):
-            stage(work, t - lag)
+        stage(over_z, t - LAGS[0])
+        stage(update, t - LAGS[2])
         for step, works in late.items():
             @pl.when(t == step)
             def _():
                 for work, k in works:
                     work(k)
+        stage(encode, t - LAGS[1])
 
     pltpu.make_async_copy(inbox, inbox, send_sem.at[0]).wait()
     pltpu.make_async_copy(last_inbox, last_inbox, send_sem.at[1]).wait()
@@ -307,7 +335,7 @@
 def per_device(params, public, mixed, hidden, cotangent):
     _, rows, width = params.shape
     _, rounds, tokens, rows_all = hidden.shape
-    items = rounds * CHUNKS - 1
+    items = rounds * CHUNKS - 2
     w = width // CHUNKS
     piece = pltpu.VMEM((items, rows, w), jnp.bfloat16)
     state = pltpu.VMEM((CHUNKS, rows, w), jnp.float32)
@@ -321,19 +349,20 @@
         scratch_shapes=[
             pltpu.VMEM((rounds, tokens, rows_all), jnp.bfloat16),
             pltpu.VMEM((rounds, rows_all, tokens), jnp.bfloat16),
-            pltpu.VMEM((items + 1, tokens, w), jnp.bfloat16),
+            pltpu.VMEM((items + 2, tokens, w), jnp.bfloat16),
             state, state, state,
             pltpu.VMEM((items, rows_all // rows, rows, w), jnp.bfloat16),
             pltpu.VMEM((items, INBOX, rows, w), jnp.bfloat16),
             *[piece] * 4,
             state, state,
             pltpu.VMEM((2 * LANES, LANES), jnp.bfloat16),
-            pltpu.VMEM((PIECES, rows_all // rows, rows, w // PIECES), jnp.bfloat16),
-            pltpu.VMEM((PIECES, INBOX, rows, w // PIECES), jnp.bfloat16),
-            pltpu.VMEM((PIECES, rows, w // PIECES), jnp.bfloat16),
-            pltpu.VMEM((PIECES, rows, w // PIECES), jnp.bfloat16),
+            pltpu.VMEM((PIECES, rows_all // rows, rows, w // 2), jnp.bfloat16),
+            pltpu.VMEM((PIECES, INBOX, rows, w // 2), jnp.bfloat16),
+            pltpu.VMEM((2, rows, w // 2), jnp.bfloat16),
+            pltpu.VMEM((2, XSIDE - 1, rows, w // 2), jnp.bfloat16),
+            pltpu.VMEM((PIECES, rows, w // 2), jnp.bfloat16),
             pltpu.SemaphoreType.DMA((1,)),
-            pltpu.SemaphoreType.DMA((items + 1,)),
+            pltpu.SemaphoreType.DMA((items + 2,)),
             pltpu.SemaphoreType.DMA((3, CHUNKS)),
             pltpu.SemaphoreType.DMA((2,)),
             pltpu.SemaphoreType.DMA((len(LANDS), items)),

time: 50.8 us -> 50.5 us (level); the launches traced: 50.1 us -> 50.3 us
  no operation moved by 1% of the time
where the time goes in v3:
time: 50.5 us; the launch traced here: 50.3 us
  Pallas kernels  49.6 us (98%)
  between operations  0.64 us (1%)
    pallas_call x1, Pallas kernels, per_device(): pl.pallas_call(kernel, out_shape=(pltpu.VMEM(params.shape, jnp.float32),)...  48.7 us

profile of v3, /device:TPU:6, one launch (start us, length us, event | category | flops | bytes accessed | tf_op | source)
XLA Modules:
  0.0 50.3 jit_solution(10739704206424353777)
XLA Ops:
  0.6 48.7 %shard_map.76 = (f32[1,16,5120]{2,1,0:T(8,128)S(1)}, f32[1,16,5120]{2,1,0:T(8,128)S(1)}, f32[1,16,5120]{2,1,0:T(8,128)S(1)}) custom-call(f32[1,16,5120]{2,1,0:T(8,128)} %par_hbm.1, f32[1,16,5120]{2,1,0:T(8,128)} %pub_hbm.1, f32[1,16,5120]{2,1,0:T(8,128)} %mix_hbm.1, bf16[1,2,128,128]{3,2,1,0:T(8,128)(2,1)} %hid_hbm.1, bf16[1,2,128,5120]{3,2,1,0:T(8,128)(2,1)} %cot_hbm.1), custom_call_target="tpu_custom_call" | custom-call | flops 340000000 | bytes 5000000 | tf_op jit(solution)/shard_map/pallas_call | solution.py:344
  49.3 1.0 %shard_map.77 = (f32[1,16,5120]{2,1,0:T(8,128)}, f32[1,16,5120]{2,1,0:T(8,128)}, f32[1,16,5120]{2,1,0:T(8,128)}) custom-call(f32[1,16,5120]{2,1,0:T(8,128)S(1)} %get-tuple-element.6.refs_0_, f32[1,16,5120]{2,1,0:T(8,128)S(1)} %get-tuple-element.7.refs_1_, f32[1,16,5120]{2,1,0:T(8,128)S(1)} %get-tuple-element.8.refs_2_), custom_call_target="tpu_custom_call" | custom-call | tf_op jit(solution)/shard_map/pallas_call | solution.py:375

commit v4 on v3

--- a/solution.py
+++ b/solution.py
@@ -14,7 +14,7 @@
 MIX_RATE = 0.4
 SCALE_FLOOR = 0.25
 CODE_LIMIT = 2.0
-CHUNKS = 4
+CHUNKS = 5
 XSIDE = 4
 AHEAD = 3
 LAGS = (2, 4, 6)
@@ -77,10 +77,15 @@
     def cols(c):
         return pl.ds(pl.multiple_of(c * w, LANES), w)
 
+    def chunk_of(t):
+        if isinstance(t, int) and t >= items:
+            return 1 - (t - items)
+        return t - t // chunks * (chunks - 2)
+
     hid_load = pltpu.make_async_copy(hid_hbm.at[0], hid, hid_sem.at[0])
 
     def cot_load(t):
-        return pltpu.make_async_copy(cot_hbm.at[0, t // chunks, :, cols(t % chunks)], cot.at[t], cot_sem.at[t])
+        return pltpu.make_async_copy(cot_hbm.at[0, t // chunks, :, cols(chunk_of(t))], cot.at[t], cot_sem.at[t])
 
     def state_loads(c):
         return [pltpu.make_async_copy(src.at[0, :, cols(c)], dst.at[c], state_sem.at[i, c])
@@ -170,7 +175,7 @@
         return step_v[c, :, columns] + MIX_RATE * (mixed - public), public, mixed
 
     def encode(t):
-        c = t % chunks
+        c = chunk_of(t)
 
         @pl.when(t < chunks)
         def _():
@@ -184,7 +189,7 @@
         start(GO_BEFORE, t)
 
     def update(t):
-        c = t % chunks
+        c = chunk_of(t)
         arrived(GOSSIP, t)
         params, public, mixed = mix_in(c, slice(0, w), add(inbox.at[t, IN_BEFORE], inbox.at[t, IN_AFTER]))
 
@@ -203,7 +208,7 @@
         return (LANDS_X_FIRST if k < 2 else LANDS_Z_FIRST)[group]
 
     def place_of(k):
-        return chunks - 2 + k // 2, slice(k % 2 * wl, k % 2 * wl + wl)
+        return 1 - k // 2, slice(k % 2 * wl, k % 2 * wl + wl)
 
     def last_start(k, src, slot, device, group):
         pltpu.make_async_remote_copy(
@@ -263,7 +268,10 @@
     pl.semaphore_wait(barrier, 6)
     send_parts(0)
 
-    @pl.loop(AHEAD, items + 2)
+    for t in (items + 1, items):
+        cot_load(t).start()
+
+    @pl.loop(AHEAD, items)
     def _(t):
         cot_load(t).start()
 
@@ -296,22 +304,22 @@
 
     late = {items - 3: ((last_send_parts, 0),), items - 2: ((last_send_parts, 1),),
             items - 1: ((late_send_parts, 2), (late_send_parts, 3)),
-            items: ((last_over_z, 0),), items + 1: ((last_over_z, 1),),
-            items + 3: ((last_encode, 0), (last_encode, 2), (last_encode, 3)), items + 4: ((last_encode, 1),),
-            items + 5: ((last_update, 0), (last_update, 2), (last_update, 3), (last_update, 1))}
+            items: ((last_over_z, 0),), items + 1: ((last_over_z, 1), (last_encode, 2), (last_encode, 3)),
+            items + 3: ((last_encode, 0), (last_encode, 1)),
+            items + 5: ((last_update, 2), (last_update, 3), (last_update, 0), (last_update, 1))}
 
     @pl.loop(0, items + LAGS[-1])
     def _(t):
         stage(pass_on, t)
         stage(send_parts, t + AHEAD)
         stage(over_z, t - LAGS[0])
-        stage(update, t - LAGS[2])
         for step, works in late.items():
             @pl.when(t == step)
             def _():
                 for work, k in works:
                     work(k)
         stage(encode, t - LAGS[1])
+        stage(update, t - LAGS[2])
 
     pltpu.make_async_copy(inbox, inbox, send_sem.at[0]).wait()
     pltpu.make_async_copy(last_inbox, last_inbox, send_sem.at[1]).wait()

time: 50.5 us -> 47.9 us (0.949)
  Pallas kernels: 49.6 us -> 46.8 us
    pallas_call x1, Pallas kernels: 48.7 us -> 45.8 us  [per_device(): pl.pallas_call(kernel, out_shape=(pltpu.VMEM(params.shape, jnp.float32),)...]
where the time goes in v4:
time: 47.9 us; the launch traced here: 47.4 us
  Pallas kernels  46.8 us (98%)
  between operations  0.64 us (1%)
    pallas_call x1, Pallas kernels, per_device(): pl.pallas_call(kernel, out_shape=(pltpu.VMEM(params.shape, jnp.float32),)...  45.8 us
    pallas_call x1, Pallas kernels, per_device(): pl.pallas_call(deliver, out_shape=(jax.ShapeDtypeStruct(params.shape, jnp...  0.99 us

profile of v4, /device:TPU:6, one launch (start us, length us, event | category | flops | bytes accessed | tf_op | source)
XLA Modules:
  0.0 47.4 jit_solution(17912360992280533656)
XLA Ops:
  0.6 45.8 %shard_map.76 = (f32[1,16,5120]{2,1,0:T(8,128)S(1)}, f32[1,16,5120]{2,1,0:T(8,128)S(1)}, f32[1,16,5120]{2,1,0:T(8,128)S(1)}) custom-call(f32[1,16,5120]{2,1,0:T(8,128)} %par_hbm.1, f32[1,16,5120]{2,1,0:T(8,128)} %pub_hbm.1, f32[1,16,5120]{2,1,0:T(8,128)} %mix_hbm.1, bf16[1,2,128,128]{3,2,1,0:T(8,128)(2,1)} %hid_hbm.1, bf16[1,2,128,5120]{3,2,1,0:T(8,128)(2,1)} %cot_hbm.1), custom_call_target="tpu_custom_call" | custom-call | flops 340000000 | bytes 5000000 | tf_op jit(solution)/shard_map/pallas_call | solution.py:352
  46.4 1.0 %shard_map.77 = (f32[1,16,5120]{2,1,0:T(8,128)}, f32[1,16,5120]{2,1,0:T(8,128)}, f32[1,16,5120]{2,1,0:T(8,128)}) custom-call(f32[1,16,5120]{2,1,0:T(8,128)S(1)} %get-tuple-element.6.refs_0_, f32[1,16,5120]{2,1,0:T(8,128)S(1)} %get-tuple-element.7.refs_1_, f32[1,16,5120]{2,1,0:T(8,128)S(1)} %get-tuple-element.8.refs_2_), custom_call_target="tpu_custom_call" | custom-call | tf_op jit(solution)/shard_map/pallas_call | solution.py:383

commit v5 on v4

--- a/solution.py
+++ b/solution.py
@@ -14,7 +14,7 @@
 MIX_RATE = 0.4
 SCALE_FLOOR = 0.25
 CODE_LIMIT = 2.0
-CHUNKS = 5
+CHUNKS = 4
 XSIDE = 4
 AHEAD = 3
 LAGS = (2, 4, 6)
@@ -304,7 +304,8 @@
 
     late = {items - 3: ((last_send_parts, 0),), items - 2: ((last_send_parts, 1),),
             items - 1: ((late_send_parts, 2), (late_send_parts, 3)),
-            items: ((last_over_z, 0),), items + 1: ((last_over_z, 1), (last_encode, 2), (last_encode, 3)),
+            items: ((last_over_z, 0),), items + 1: ((last_over_z, 1),),
+            items + 2: ((last_encode, 2), (last_encode, 3)),
             items + 3: ((last_encode, 0), (last_encode, 1)),
             items + 5: ((last_update, 2), (last_update, 3), (last_update, 0), (last_update, 1))}
 
@@ -318,8 +319,8 @@
             def _():
                 for work, k in works:
                     work(k)
+        stage(update, t - LAGS[2])
         stage(encode, t - LAGS[1])
-        stage(update, t - LAGS[2])
 
     pltpu.make_async_copy(inbox, inbox, send_sem.at[0]).wait()
     pltpu.make_async_copy(last_inbox, last_inbox, send_sem.at[1]).wait()
@@ -330,9 +331,9 @@
     arrays = (len(refs) - 1) // 2
     copies = []
     for i in range(arrays):
-        half = refs[i].shape[1] // 2
-        for j in range(2):
-            piece = (0, pl.ds(j * half, half))
+        half, part = refs[i].shape[1] // 2, refs[i].shape[2] // 2
+        for j in range(4):
+            piece = (0, pl.ds(j // 2 * half, half), pl.ds(j % 2 * part, part))
             copies.append(pltpu.make_async_copy(refs[i].at[piece], refs[arrays + i].at[piece], sem.at[i, j]))
     for copy in copies:
         copy.start()
@@ -385,7 +386,7 @@
         out_shape=(jax.ShapeDtypeStruct(params.shape, jnp.float32),) * 3,
         in_specs=[in_vmem] * 3,
         out_specs=(anywhere,) * 3,
-        scratch_shapes=[pltpu.SemaphoreType.DMA((3, 2))],
+        scratch_shapes=[pltpu.SemaphoreType.DMA((3, 4))],
         compiler_params=pltpu.CompilerParams(vmem_limit_bytes=1024 * 1024),
     )(*[pltpu.with_memory_space_constraint(a, pltpu.VMEM) for a in results])
 

time: 47.9 us -> 48.9 us (1.021)
  Pallas kernels: 46.8 us -> 47.8 us
    pallas_call x1, Pallas kernels: 45.8 us -> 46.7 us  [per_device(): pl.pallas_call(kernel, out_shape=(pltpu.VMEM(params.shape, jnp.float32),)...]
where the time goes in v5:
time: 48.9 us; the launch traced here: 48.4 us
  Pallas kernels  47.8 us (98%)
  between operations  0.64 us (1%)
    pallas_call x1, Pallas kernels, per_device(): pl.pallas_call(kernel, out_shape=(pltpu.VMEM(params.shape, jnp.float32),)...  46.7 us
    pallas_call x1, Pallas kernels, per_device(): pl.pallas_call(deliver, out_shape=(jax.ShapeDtypeStruct(params.shape, jnp...  1.04 us

profile of v5, /device:TPU:6, one launch (start us, length us, event | category | flops | bytes accessed | tf_op | source)
XLA Modules:
  0.0 48.4 jit_solution(16275818385016899553)
XLA Ops:
  0.6 46.7 %shard_map.76 = (f32[1,16,5120]{2,1,0:T(8,128)S(1)}, f32[1,16,5120]{2,1,0:T(8,128)S(1)}, f32[1,16,5120]{2,1,0:T(8,128)S(1)}) custom-call(f32[1,16,5120]{2,1,0:T(8,128)} %par_hbm.1, f32[1,16,5120]{2,1,0:T(8,128)} %pub_hbm.1, f32[1,16,5120]{2,1,0:T(8,128)} %mix_hbm.1, bf16[1,2,128,128]{3,2,1,0:T(8,128)(2,1)} %hid_hbm.1, bf16[1,2,128,5120]{3,2,1,0:T(8,128)(2,1)} %cot_hbm.1), custom_call_target="tpu_custom_call" | custom-call | flops 340000000 | bytes 5000000 | tf_op jit(solution)/shard_map/pallas_call | solution.py:353
  47.4 1.0 %shard_map.77 = (f32[1,16,5120]{2,1,0:T(8,128)}, f32[1,16,5120]{2,1,0:T(8,128)}, f32[1,16,5120]{2,1,0:T(8,128)}) custom-call(f32[1,16,5120]{2,1,0:T(8,128)S(1)} %get-tuple-element.6.refs_0_, f32[1,16,5120]{2,1,0:T(8,128)S(1)} %get-tuple-element.7.refs_1_, f32[1,16,5120]{2,1,0:T(8,128)S(1)} %get-tuple-element.8.refs_2_), custom_call_target="tpu_custom_call" | custom-call | tf_op jit(solution)/shard_map/pallas_call | solution.py:384

commit v6 on v4

--- a/solution.py
+++ b/solution.py
@@ -17,7 +17,7 @@
 CHUNKS = 5
 XSIDE = 4
 AHEAD = 3
-LAGS = (2, 4, 6)
+LAGS = (2, 5, 7)
 
 TO_RIGHT, TO_LEFT, SUM_O, SUM_M, OVER, GO_AFTER, GO_BEFORE = range(7)
 PARTS, SUMS, ACROSS, GOSSIP = range(4)
@@ -70,10 +70,6 @@
     after = ((b + 1) % nb, f)
     before = ((b + nb - 1) % nb, f)
 
-    barrier = pltpu.get_barrier_semaphore()
-    for device in (right, left, opposite, across, after, before):
-        pl.semaphore_signal(barrier, inc=1, device_id=device, device_id_type=MESH)
-
     def cols(c):
         return pl.ds(pl.multiple_of(c * w, LANES), w)
 
@@ -91,9 +87,18 @@
         return [pltpu.make_async_copy(src.at[0, :, cols(c)], dst.at[c], state_sem.at[i, c])
                 for i, (src, dst) in enumerate(((par_hbm, par), (pub_hbm, pub), (mix_hbm, mix)))]
 
+    def first_loads():
+        step = tokens // 4
+        return [pltpu.make_async_copy(cot_hbm.at[0, 0, pl.ds(i * step, step), pl.ds(0, w)],
+                                      cot.at[0, pl.ds(i * step, step)], hid_sem.at[1 + i]) for i in range(4)]
+
     hid_load.start()
-    for t in range(AHEAD):
-        cot_load(t).start()
+    for copy in first_loads():
+        copy.start()
+
+    barrier = pltpu.get_barrier_semaphore()
+    for device in (right, left, opposite, across, after, before):
+        pl.semaphore_signal(barrier, inc=1, device_id=device, device_id_type=MESH)
 
     def land(t, first, blocks=1):
         return inbox.at[t, pl.ds(first, blocks)]
@@ -119,7 +124,11 @@
     places = [3 * ((j // 2 + XSIDE - x) % XSIDE * 2 + (j + zh) % 2) % 8 for j in range(rows_all // rows)]
 
     def product(t):
-        cot_load(t).wait()
+        if not isinstance(t, int) or t > 0:
+            cot_load(t).wait()
+        else:
+            for copy in first_loads():
+                copy.wait()
         return jnp.dot(hid_t[t // chunks], cot[t], preferred_element_type=jnp.float32).astype(jnp.bfloat16)
 
     def multiply(t):
@@ -268,7 +277,7 @@
     pl.semaphore_wait(barrier, 6)
     send_parts(0)
 
-    for t in (items + 1, items):
+    for t in (*range(1, AHEAD), items + 1, items):
         cot_load(t).start()
 
     @pl.loop(AHEAD, items)
@@ -304,9 +313,10 @@
 
     late = {items - 3: ((last_send_parts, 0),), items - 2: ((last_send_parts, 1),),
             items - 1: ((late_send_parts, 2), (late_send_parts, 3)),
-            items: ((last_over_z, 0),), items + 1: ((last_over_z, 1), (last_encode, 2), (last_encode, 3)),
+            items: ((last_over_z, 0),), items + 1: ((last_over_z, 1),),
+            items + 2: ((last_encode, 2), (last_encode, 3)),
             items + 3: ((last_encode, 0), (last_encode, 1)),
-            items + 5: ((last_update, 2), (last_update, 3), (last_update, 0), (last_update, 1))}
+            items + 6: ((last_update, 2), (last_update, 3), (last_update, 0), (last_update, 1))}
 
     @pl.loop(0, items + LAGS[-1])
     def _(t):
@@ -369,7 +379,7 @@
             pltpu.VMEM((2, rows, w // 2), jnp.bfloat16),
             pltpu.VMEM((2, XSIDE - 1, rows, w // 2), jnp.bfloat16),
             pltpu.VMEM((PIECES, rows, w // 2), jnp.bfloat16),
-            pltpu.SemaphoreType.DMA((1,)),
+            pltpu.SemaphoreType.DMA((5,)),
             pltpu.SemaphoreType.DMA((items + 2,)),
             pltpu.SemaphoreType.DMA((3, CHUNKS)),
             pltpu.SemaphoreType.DMA((2,)),

time: 47.9 us -> 50.4 us (1.052)
  Pallas kernels: 46.8 us -> 49.5 us
    pallas_call x1, Pallas kernels: 45.8 us -> 48.5 us  [per_device(): pl.pallas_call(kernel, out_shape=(pltpu.VMEM(params.shape, jnp.float32),)...]
where the time goes in v6:
time: 50.4 us; the launch traced here: 50.2 us
  Pallas kernels  49.5 us (98%)
  between operations  0.64 us (1%)
    pallas_call x1, Pallas kernels, per_device(): pl.pallas_call(kernel, out_shape=(pltpu.VMEM(params.shape, jnp.float32),)...  48.5 us

profile of v6, /device:TPU:6, one launch (start us, length us, event | category | flops | bytes accessed | tf_op | source)
XLA Modules:
  0.0 50.2 jit_solution(10656685721992207079)
XLA Ops:
  0.6 48.5 %shard_map.76 = (f32[1,16,5120]{2,1,0:T(8,128)S(1)}, f32[1,16,5120]{2,1,0:T(8,128)S(1)}, f32[1,16,5120]{2,1,0:T(8,128)S(1)}) custom-call(f32[1,16,5120]{2,1,0:T(8,128)} %par_hbm.1, f32[1,16,5120]{2,1,0:T(8,128)} %pub_hbm.1, f32[1,16,5120]{2,1,0:T(8,128)} %mix_hbm.1, bf16[1,2,128,128]{3,2,1,0:T(8,128)(2,1)} %hid_hbm.1, bf16[1,2,128,5120]{3,2,1,0:T(8,128)(2,1)} %cot_hbm.1), custom_call_target="tpu_custom_call" | custom-call | flops 340000000 | bytes 5000000 | tf_op jit(solution)/shard_map/pallas_call | solution.py:362
  49.2 1.0 %shard_map.77 = (f32[1,16,5120]{2,1,0:T(8,128)}, f32[1,16,5120]{2,1,0:T(8,128)}, f32[1,16,5120]{2,1,0:T(8,128)}) custom-call(f32[1,16,5120]{2,1,0:T(8,128)S(1)} %get-tuple-element.6.refs_0_, f32[1,16,5120]{2,1,0:T(8,128)S(1)} %get-tuple-element.7.refs_1_, f32[1,16,5120]{2,1,0:T(8,128)S(1)} %get-tuple-element.8.refs_2_), custom_call_target="tpu_custom_call" | custom-call | tf_op jit(solution)/shard_map/pallas_call | solution.py:393

commit v7 on v6

--- a/solution.py
+++ b/solution.py
@@ -17,7 +17,8 @@
 CHUNKS = 5
 XSIDE = 4
 AHEAD = 3
-LAGS = (2, 5, 7)
+EARLY = 5
+LAGS = (2, 4, 6)
 
 TO_RIGHT, TO_LEFT, SUM_O, SUM_M, OVER, GO_AFTER, GO_BEFORE = range(7)
 PARTS, SUMS, ACROSS, GOSSIP = range(4)
@@ -300,23 +301,19 @@
     early_over_z(2)
     early_over_z(3)
 
-    @pl.loop(AHEAD, items)
-    def _(t):
+    for t in range(AHEAD, EARLY):
         multiply(t)
-
-    multiply_last(0)
 
     def stage(work, item):
         @pl.when((item >= 0) & (item < items))
         def _():
             work(item)
 
-    late = {items - 3: ((last_send_parts, 0),), items - 2: ((last_send_parts, 1),),
+    late = {2: ((multiply_last, 0),), items - 3: ((last_send_parts, 0),), items - 2: ((last_send_parts, 1),),
             items - 1: ((late_send_parts, 2), (late_send_parts, 3)),
-            items: ((last_over_z, 0),), items + 1: ((last_over_z, 1),),
-            items + 2: ((last_encode, 2), (last_encode, 3)),
+            items: ((last_over_z, 0),), items + 1: ((last_over_z, 1), (last_encode, 2), (last_encode, 3)),
             items + 3: ((last_encode, 0), (last_encode, 1)),
-            items + 6: ((last_update, 2), (last_update, 3), (last_update, 0), (last_update, 1))}
+            items + 5: ((last_update, 2), (last_update, 3), (last_update, 0), (last_update, 1))}
 
     @pl.loop(0, items + LAGS[-1])
     def _(t):
@@ -330,6 +327,7 @@
                     work(k)
         stage(encode, t - LAGS[1])
         stage(update, t - LAGS[2])
+        stage(multiply, t + EARLY)
 
     pltpu.make_async_copy(inbox, inbox, send_sem.at[0]).wait()
     pltpu.make_async_copy(last_inbox, last_inbox, send_sem.at[1]).wait()

time: 50.4 us -> 47.5 us (0.942)
  the two profiles are of different devices: /device:TPU:6 before, /device:TPU:1 now
where the time goes in v7:
time: 47.5 us; the launch traced here: 47.4 us
  Pallas kernels  46.7 us (98%)
  between operations  0.64 us (1%)
    pallas_call x1, Pallas kernels, per_device(): pl.pallas_call(kernel, out_shape=(pltpu.VMEM(params.shape, jnp.float32),)...  45.7 us
    pallas_call x1, Pallas kernels, per_device(): pl.pallas_call(deliver, out_shape=(jax.ShapeDtypeStruct(params.shape, jnp...  0.99 us

profile of v7, /device:TPU:1, one launch (start us, length us, event | category | flops | bytes accessed | tf_op | source)
XLA Modules:
  0.0 47.4 jit_solution(10153176322047689235)
XLA Ops:
  0.6 45.7 %shard_map.76 = (f32[1,16,5120]{2,1,0:T(8,128)S(1)}, f32[1,16,5120]{2,1,0:T(8,128)S(1)}, f32[1,16,5120]{2,1,0:T(8,128)S(1)}) custom-call(f32[1,16,5120]{2,1,0:T(8,128)} %par_hbm.1, f32[1,16,5120]{2,1,0:T(8,128)} %pub_hbm.1, f32[1,16,5120]{2,1,0:T(8,128)} %mix_hbm.1, bf16[1,2,128,128]{3,2,1,0:T(8,128)(2,1)} %hid_hbm.1, bf16[1,2,128,5120]{3,2,1,0:T(8,128)(2,1)} %cot_hbm.1), custom_call_target="tpu_custom_call" | custom-call | flops 340000000 | bytes 5000000 | tf_op jit(solution)/shard_map/pallas_call | solution.py:360
  46.4 1.0 %shard_map.77 = (f32[1,16,5120]{2,1,0:T(8,128)}, f32[1,16,5120]{2,1,0:T(8,128)}, f32[1,16,5120]{2,1,0:T(8,128)}) custom-call(f32[1,16,5120]{2,1,0:T(8,128)S(1)} %get-tuple-element.6.refs_0_, f32[1,16,5120]{2,1,0:T(8,128)S(1)} %get-tuple-element.7.refs_1_, f32[1,16,5120]{2,1,0:T(8,128)S(1)} %get-tuple-element.8.refs_2_), custom_call_target="tpu_custom_call" | custom-call | tf_op jit(solution)/shard_map/pallas_call | solution.py:391

commit v8 on v7

--- a/solution.py
+++ b/solution.py
@@ -20,11 +20,11 @@
 EARLY = 5
 LAGS = (2, 4, 6)
 
-TO_RIGHT, TO_LEFT, SUM_O, SUM_M, OVER, GO_AFTER, GO_BEFORE = range(7)
+TO_RIGHT, TO_LEFT, SUM_O, SUM_M, OVER, GO_FAR, GO_NEAR = range(7)
 PARTS, SUMS, ACROSS, GOSSIP = range(4)
 LANDS = ((0, 4), (4, 2), (6, 1), (7, 2))
 INBOX = 9
-NEAR_M, FAR_O, FAR_M, NEAR_O, IN_SUM_O, IN_SUM_M, IN_ACROSS, IN_BEFORE, IN_AFTER = range(INBOX)
+NEAR_M, FAR_O, FAR_M, NEAR_O, IN_SUM_O, IN_SUM_M, IN_ACROSS, IN_FAR, IN_NEAR = range(INBOX)
 
 PIECES = 4
 LANDS_X_FIRST = {PARTS: (0, 6), ACROSS: (6, 1), GOSSIP: (7, 2)}
@@ -68,8 +68,9 @@
     left = (b, (x + XSIDE - 1) % XSIDE * 2 + zh)
     across = (b, x * 2 + 1 - zh)
     opposite = (b, (x + 2) % XSIDE * 2 + zh)
-    after = ((b + 1) % nb, f)
-    before = ((b + nb - 1) % nb, f)
+    core = b % 2
+    far = ((b + nb - 1 + 2 * core) % nb, f)
+    near = (b + 1 - 2 * core, f)
 
     def cols(c):
         return pl.ds(pl.multiple_of(c * w, LANES), w)
@@ -98,7 +99,7 @@
         copy.start()
 
     barrier = pltpu.get_barrier_semaphore()
-    for device in (right, left, opposite, across, after, before):
+    for device in (right, left, opposite, across, far, near):
         pl.semaphore_signal(barrier, inc=1, device_id=device, device_id_type=MESH)
 
     def land(t, first, blocks=1):
@@ -111,8 +112,8 @@
             SUM_O: lambda: (fwd_o.at[pl.ds(t, 1)], land(t, IN_SUM_O), right, SUMS),
             SUM_M: lambda: (fwd_m.at[pl.ds(t, 1)], land(t, IN_SUM_M), left, SUMS),
             OVER: lambda: (zout.at[pl.ds(t, 1)], land(t, IN_ACROSS), across, ACROSS),
-            GO_AFTER: lambda: (gout.at[pl.ds(t, 1)], land(t, IN_BEFORE), after, GOSSIP),
-            GO_BEFORE: lambda: (gout.at[pl.ds(t, 1)], land(t, IN_AFTER), before, GOSSIP),
+            GO_FAR: lambda: (gout.at[pl.ds(t, 1)], land(t, IN_FAR), far, GOSSIP),
+            GO_NEAR: lambda: (gout.at[pl.ds(t, 1)], land(t, IN_NEAR), near, GOSSIP),
         }[kind]()
         pltpu.make_async_remote_copy(
             src_ref=src, dst_ref=dst, send_sem=send_sem.at[0], recv_sem=recv_sem.at[group, t],
@@ -195,13 +196,13 @@
         arrived(ACROSS, t)
         gradient = add(part.at[t, OWN_MINE], inbox.at[t, NEAR_M], inbox.at[t, IN_SUM_M], inbox.at[t, IN_ACROSS])
         gout[t] = code(c, slice(0, w), gradient)
-        start(GO_AFTER, t)
-        start(GO_BEFORE, t)
+        start(GO_FAR, t)
+        start(GO_NEAR, t)
 
     def update(t):
         c = chunk_of(t)
         arrived(GOSSIP, t)
-        params, public, mixed = mix_in(c, slice(0, w), add(inbox.at[t, IN_BEFORE], inbox.at[t, IN_AFTER]))
+        params, public, mixed = mix_in(c, slice(0, w), add(inbox.at[t, IN_FAR], inbox.at[t, IN_NEAR]))
 
         @pl.when(t < (rounds - 1) * chunks)
         def _():
@@ -256,8 +257,8 @@
         c, columns = place_of(k)
         last_gout[k] = code(c, columns, gradient)
         first = lands(GOSSIP, k)[0]
-        last_start(k, last_gout.at[pl.ds(k, 1)], first, after, GOSSIP)
-        last_start(k, last_gout.at[pl.ds(k, 1)], first + 1, before, GOSSIP)
+        last_start(k, last_gout.at[pl.ds(k, 1)], first, far, GOSSIP)
+        last_start(k, last_gout.at[pl.ds(k, 1)], first + 1, near, GOSSIP)
 
     def last_update(k):
         last_arrived(GOSSIP, k)

time: 47.5 us -> 47.5 us (level)
  no operation moved by 1% of the time
where the time goes in v8:
time: 47.5 us; the launch traced here: 47.4 us
  Pallas kernels  46.7 us (98%)
  between operations  0.64 us (1%)
    pallas_call x1, Pallas kernels, per_device(): pl.pallas_call(kernel, out_shape=(pltpu.VMEM(params.shape, jnp.float32),)...  45.7 us
    pallas_call x1, Pallas kernels, per_device(): pl.pallas_call(deliver, out_shape=(jax.ShapeDtypeStruct(params.shape, jnp...  0.99 us

profile of v8, /device:TPU:1, one launch (start us, length us, event | category | flops | bytes accessed | tf_op | source)
XLA Modules:
  0.0 47.4 jit_solution(5095576493077006656)
XLA Ops:
  0.6 45.7 %shard_map.76 = (f32[1,16,5120]{2,1,0:T(8,128)S(1)}, f32[1,16,5120]{2,1,0:T(8,128)S(1)}, f32[1,16,5120]{2,1,0:T(8,128)S(1)}) custom-call(f32[1,16,5120]{2,1,0:T(8,128)} %par_hbm.1, f32[1,16,5120]{2,1,0:T(8,128)} %pub_hbm.1, f32[1,16,5120]{2,1,0:T(8,128)} %mix_hbm.1, bf16[1,2,128,128]{3,2,1,0:T(8,128)(2,1)} %hid_hbm.1, bf16[1,2,128,5120]{3,2,1,0:T(8,128)(2,1)} %cot_hbm.1), custom_call_target="tpu_custom_call" | custom-call | flops 340000000 | bytes 5000000 | tf_op jit(solution)/shard_map/pallas_call | solution.py:361
  46.4 1.0 %shard_map.77 = (f32[1,16,5120]{2,1,0:T(8,128)}, f32[1,16,5120]{2,1,0:T(8,128)}, f32[1,16,5120]{2,1,0:T(8,128)}) custom-call(f32[1,16,5120]{2,1,0:T(8,128)S(1)} %get-tuple-element.6.refs_0_, f32[1,16,5120]{2,1,0:T(8,128)S(1)} %get-tuple-element.7.refs_1_, f32[1,16,5120]{2,1,0:T(8,128)S(1)} %get-tuple-element.8.refs_2_), custom_call_target="tpu_custom_call" | custom-call | tf_op jit(solution)/shard_map/pallas_call | solution.py:392

commit v9 on v8

--- a/solution.py
+++ b/solution.py
@@ -310,10 +310,10 @@
         def _():
             work(item)
 
-    late = {2: ((multiply_last, 0),), items - 3: ((last_send_parts, 0),), items - 2: ((last_send_parts, 1),),
-            items - 1: ((late_send_parts, 2), (late_send_parts, 3)),
+    late = {2: ((multiply_last, 0),), items - 3: ((last_send_parts, 0),),
+            items - 1: ((last_send_parts, 1), (late_send_parts, 2), (late_send_parts, 3)),
             items: ((last_over_z, 0),), items + 1: ((last_over_z, 1), (last_encode, 2), (last_encode, 3)),
-            items + 3: ((last_encode, 0), (last_encode, 1)),
+            items + 3: ((last_encode, 0),), items + 4: ((last_encode, 1),),
             items + 5: ((last_update, 2), (last_update, 3), (last_update, 0), (last_update, 1))}
 
     @pl.loop(0, items + LAGS[-1])

time: 47.5 us -> 48 us (1.011)
  the two profiles are of different devices: /device:TPU:1 before, /device:TPU:2 now
where the time goes in v9:
time: 48 us; the launch traced here: 47.8 us
  Pallas kernels  47.2 us (98%)
  between operations  0.64 us (1%)
    pallas_call x1, Pallas kernels, per_device(): pl.pallas_call(kernel, out_shape=(pltpu.VMEM(params.shape, jnp.float32),)...  46.2 us
    pallas_call x1, Pallas kernels, per_device(): pl.pallas_call(deliver, out_shape=(jax.ShapeDtypeStruct(params.shape, jnp...  0.99 us

profile of v9, /device:TPU:2, one launch (start us, length us, event | category | flops | bytes accessed | tf_op | source)
XLA Modules:
  0.0 47.8 jit_solution(15404112522400780557)
XLA Ops:
  0.6 46.2 %shard_map.76 = (f32[1,16,5120]{2,1,0:T(8,128)S(1)}, f32[1,16,5120]{2,1,0:T(8,128)S(1)}, f32[1,16,5120]{2,1,0:T(8,128)S(1)}) custom-call(f32[1,16,5120]{2,1,0:T(8,128)} %par_hbm.1, f32[1,16,5120]{2,1,0:T(8,128)} %pub_hbm.1, f32[1,16,5120]{2,1,0:T(8,128)} %mix_hbm.1, bf16[1,2,128,128]{3,2,1,0:T(8,128)(2,1)} %hid_hbm.1, bf16[1,2,128,5120]{3,2,1,0:T(8,128)(2,1)} %cot_hbm.1), custom_call_target="tpu_custom_call" | custom-call | flops 340000000 | bytes 5000000 | tf_op jit(solution)/shard_map/pallas_call | solution.py:361
  46.8 1.0 %shard_map.77 = (f32[1,16,5120]{2,1,0:T(8,128)}, f32[1,16,5120]{2,1,0:T(8,128)}, f32[1,16,5120]{2,1,0:T(8,128)}) custom-call(f32[1,16,5120]{2,1,0:T(8,128)S(1)} %get-tuple-element.6.refs_0_, f32[1,16,5120]{2,1,0:T(8,128)S(1)} %get-tuple-element.7.refs_1_, f32[1,16,5120]{2,1,0:T(8,128)S(1)} %get-tuple-element.8.refs_2_), custom_call_target="tpu_custom_call" | custom-call | tf_op jit(solution)/shard_map/pallas_call | solution.py:392

commit v10 on v8

--- a/solution.py
+++ b/solution.py
@@ -16,7 +16,7 @@
 CODE_LIMIT = 2.0
 CHUNKS = 5
 XSIDE = 4
-AHEAD = 3
+AHEAD = 4
 EARLY = 5
 LAGS = (2, 4, 6)
 

time: 47.5 us -> 49 us (1.032)
  the two profiles are of different devices: /device:TPU:1 before, /device:TPU:2 now
where the time goes in v10:
time: 49 us; the launch traced here: 48.8 us
  Pallas kernels  48.2 us (98%)
  between operations  0.64 us (1%)
    pallas_call x1, Pallas kernels, per_device(): pl.pallas_call(kernel, out_shape=(pltpu.VMEM(params.shape, jnp.float32),)...  47.2 us
    pallas_call x1, Pallas kernels, per_device(): pl.pallas_call(deliver, out_shape=(jax.ShapeDtypeStruct(params.shape, jnp...  0.99 us

profile of v10, /device:TPU:2, one launch (start us, length us, event | category | flops | bytes accessed | tf_op | source)
XLA Modules:
  0.0 48.8 jit_solution(6736778703682615930)
XLA Ops:
  0.6 47.2 %shard_map.76 = (f32[1,16,5120]{2,1,0:T(8,128)S(1)}, f32[1,16,5120]{2,1,0:T(8,128)S(1)}, f32[1,16,5120]{2,1,0:T(8,128)S(1)}) custom-call(f32[1,16,5120]{2,1,0:T(8,128)} %par_hbm.1, f32[1,16,5120]{2,1,0:T(8,128)} %pub_hbm.1, f32[1,16,5120]{2,1,0:T(8,128)} %mix_hbm.1, bf16[1,2,128,128]{3,2,1,0:T(8,128)(2,1)} %hid_hbm.1, bf16[1,2,128,5120]{3,2,1,0:T(8,128)(2,1)} %cot_hbm.1), custom_call_target="tpu_custom_call" | custom-call | flops 340000000 | bytes 5000000 | tf_op jit(solution)/shard_map/pallas_call | solution.py:361
  47.9 1.0 %shard_map.77 = (f32[1,16,5120]{2,1,0:T(8,128)}, f32[1,16,5120]{2,1,0:T(8,128)}, f32[1,16,5120]{2,1,0:T(8,128)}) custom-call(f32[1,16,5120]{2,1,0:T(8,128)S(1)} %get-tuple-element.6.refs_0_, f32[1,16,5120]{2,1,0:T(8,128)S(1)} %get-tuple-element.7.refs_1_, f32[1,16,5120]{2,1,0:T(8,128)S(1)} %get-tuple-element.8.refs_2_), custom_call_target="tpu_custom_call" | custom-call | tf_op jit(solution)/shard_map/pallas_call | solution.py:392
